TPU v7x, 256 devices: a whole 4x4x8 slice. The times are simulated.
256 devices in a mesh: seq: 64 (over x, z, y_lo), head: 4 (over y_hi, core).
Axes of the slice: x: 4, y: 4 (y_hi: 2, y_lo: 2; y = y_hi * 2 + y_lo), z: 8, core: 2. Of those that a mesh axis runs over, the one named last changes fastest.
Arguments:
- queries: bfloat16 [16384, 2048], P('seq', 'head'), may hold values from -150 to 150
- keys: bfloat16 [16384, 2048], P('seq', 'head'), may hold values from -6 to 6
- values: bfloat16 [16384, 2048], P('seq', 'head'), may hold values from -8 to 8
- out_grad: bfloat16 [16384, 2048], P(('seq', 'head')), may hold values from -96 to 96
Outputs:
- query_grad: bfloat16 [16384, 2048], P('seq', 'head')
- key_grad: bfloat16 [16384, 2048], P('seq', 'head')
- value_grad: bfloat16 [16384, 2048], P('seq', 'head')
All inputs are finite; a program needn't handle non-finite values.
Results may differ from a plain program's by a relative error of at most 0.03.
Values may be sent and summed in bfloat16 or wider, within the bound.
A program may use at most 64 MiB of HBM per device.

v0:
```python
import math

import jax
import jax.numpy as jnp
from jax import lax
from jax.sharding import PartitionSpec as P

HEAD_DIM = 128
STRIDE = 256


NEG_LARGE = -1e30


def from_behind(value, axis, steps):
    count = lax.axis_size(axis)
    initial, last = (max(0, -steps), min(count, count - steps))
    return lax.ppermute(value, axis, [(source, source + steps) for source in range(initial, last)])


def split_heads(matrix):
    return matrix.reshape(matrix.shape[:-1] + (-1, HEAD_DIM))


def band_allowed(query_rows, first_row, rank_seq, length):
    query_pos = jnp.arange(query_rows)[:, None]
    key_pos = jnp.arange(query_rows + STRIDE)[None, :]
    inside = (key_pos > query_pos) & (key_pos <= query_pos + STRIDE)
    return inside & (rank_seq * length + first_row + key_pos - STRIDE >= 0)


def local_score_matrix(query_rows, key_rows, allowed):
    scores = jnp.einsum(
        "qhd,khd->hqk",
        split_heads(query_rows),
        split_heads(key_rows),
        preferred_element_type=jnp.float32,
    )
    return jnp.where(allowed[None], scores * HEAD_DIM ** (-0.5), NEG_LARGE)


def merge_lse(max_one, sum_one, max_two, sum_two):
    top = jnp.maximum(max_one, max_two)
    return top + jnp.log(sum_one * jnp.exp(max_one - top) + sum_two * jnp.exp(max_two - top))


def per_device(queries, keys, values, out_grad):
    length, width_local = queries.shape
    heads_local = width_local // HEAD_DIM
    padding_multiple = HEAD_DIM ** (-0.5)
    rank_seq = lax.axis_index("seq")
    seq_count = lax.axis_size("seq")
    grads_out = lax.all_to_all(out_grad, "head", split_axis=1, concat_axis=0, tiled=True)
    key_tail = jnp.stack([keys, values])
    earlier = from_behind(key_tail, "seq", 1)
    ext_keys = jnp.concatenate([earlier[0], keys], 0)
    ext_values = jnp.concatenate([earlier[1], values], 0)
    block_rows = math.gcd(length, 512)
    first_rows = list(range(0, length, block_rows))
    allowed_all = [
        band_allowed(block_rows, first_row, rank_seq, length) for first_row in first_rows
    ]
    stacked = jnp.stack([queries, keys, values, grads_out]).reshape(
        4, length // STRIDE, STRIDE, width_local
    )
    classes = lax.all_to_all(stacked, "seq", split_axis=2, concat_axis=1, tiled=True)
    class_q = split_heads(classes[0])
    class_k = split_heads(classes[1])
    class_v = split_heads(classes[2])
    class_g = split_heads(classes[3])
    class_blocks = class_q.shape[0]
    class_ok = (jnp.arange(class_blocks)[None, :] < jnp.arange(class_blocks)[:, None])[:, None, :]
    band_max_list = []
    band_sum_list = []
    for index, first_row in enumerate(first_rows):
        allowed = allowed_all[index]
        scores = local_score_matrix(queries, ext_keys, allowed)
        row_max = jnp.max(scores, -1)
        band_max_list.append(row_max)
        band_sum_list.append(
            jnp.sum(jnp.where(allowed[None], jnp.exp(scores - row_max[..., None]), 0.0), -1)
        )
    band_max = band_max_list[0].reshape(heads_local, length // STRIDE, STRIDE)
    band_sum = band_sum_list[0].reshape(heads_local, length // STRIDE, STRIDE)
    class_scores = (
        jnp.einsum("prhd,qrhd->hprq", class_q, class_k, preferred_element_type=jnp.float32)
        * padding_multiple
    )
    class_scores = jnp.where(class_ok[None], class_scores, NEG_LARGE)
    class_max = jnp.max(class_scores, -1)
    class_sum = jnp.sum(
        jnp.where(class_ok[None], jnp.exp(class_scores - class_max[..., None]), 0.0), -1
    )
    max_home, sum_home = (
        lax.all_to_all(class_max, "seq", split_axis=1, concat_axis=2, tiled=True),
        lax.all_to_all(class_sum, "seq", split_axis=1, concat_axis=2, tiled=True),
    )
    lse_home = merge_lse(band_max, band_sum, max_home, sum_home)
    lse_class = lax.all_to_all(lse_home, "seq", split_axis=2, concat_axis=1, tiled=True)
    lse_rows = lse_home.reshape(heads_local, length)

    def band_terms(index, first_row):
        allowed = allowed_all[index]
        stop_row = first_row + block_rows
        scores = local_score_matrix(queries, ext_keys, allowed)
        probs = jnp.where(
            allowed[None], jnp.exp(scores - lse_rows[:, first_row:stop_row, None]), 0.0
        )
        prob_grad = jnp.einsum(
            "qhd,khd->hqk",
            split_heads(grads_out),
            split_heads(ext_values),
            preferred_element_type=jnp.float32,
        )
        return (probs, prob_grad)

    band_delta_list = []
    for index, first_row in enumerate(first_rows):
        probs, prob_grad = band_terms(index, first_row)
        band_delta_list.append(jnp.sum(probs * prob_grad, -1))
    band_delta = band_delta_list[0].reshape(heads_local, length // STRIDE, STRIDE)
    class_probs = jnp.where(class_ok[None], jnp.exp(class_scores - lse_class[..., None]), 0.0)
    class_pgrad = jnp.einsum(
        "prhd,qrhd->hprq", class_g, class_v, preferred_element_type=jnp.float32
    )
    class_delta = jnp.sum(class_probs * class_pgrad, -1)
    delta_home_part = lax.all_to_all(class_delta, "seq", split_axis=1, concat_axis=2, tiled=True)
    delta_home = band_delta + delta_home_part
    delta_class = lax.all_to_all(delta_home, "seq", split_axis=2, concat_axis=1, tiled=True)
    delta_rows = delta_home.reshape(heads_local, length)
    class_sgrad = (class_probs * (class_pgrad - delta_class[..., None])).astype(jnp.bfloat16)
    class_half = class_probs.astype(jnp.bfloat16)
    class_dk = (
        jnp.einsum("hprq,prhd->qrhd", class_sgrad, class_q, preferred_element_type=jnp.float32)
        * padding_multiple
    )
    class_dv = jnp.einsum(
        "hprq,prhd->qrhd", class_half, class_g, preferred_element_type=jnp.float32
    )
    class_dq = (
        jnp.einsum("hprq,qrhd->prhd", class_sgrad, class_k, preferred_element_type=jnp.float32)
        * padding_multiple
    )
    class_grads = jnp.stack([class_dq, class_dk, class_dv]).reshape(
        3, class_blocks, STRIDE // seq_count, width_local
    )
    all_home = (
        lax.all_to_all(
            class_grads.astype(jnp.bfloat16), "seq", split_axis=1, concat_axis=2, tiled=True
        )
        .astype(class_grads.dtype)
        .reshape(3, length, width_local)
    )
    returned = (all_home[0], all_home[1], all_home[2])
    query_parts = []
    extended_key_gradient = jnp.zeros((length + STRIDE, width_local), jnp.float32)
    extended_value_gradient = jnp.zeros((length + STRIDE, width_local), jnp.float32)
    for index, first_row in enumerate(first_rows):
        stop_row = first_row + block_rows
        probs, prob_grad = band_terms(index, first_row)
        score_grad = (probs * (prob_grad - delta_rows[:, first_row:stop_row, None])).astype(
            jnp.bfloat16
        )
        prob_half = probs.astype(jnp.bfloat16)
        query_part = (
            jnp.einsum(
                "hqk,khd->qhd",
                score_grad,
                split_heads(ext_keys),
                preferred_element_type=jnp.float32,
            )
            * padding_multiple
        )
        query_parts.append(query_part.reshape(block_rows, width_local))
        key_part = (
            jnp.einsum(
                "hqk,qhd->khd", score_grad, split_heads(queries), preferred_element_type=jnp.float32
            )
            * padding_multiple
        )
        value_part = jnp.einsum(
            "hqk,qhd->khd", prob_half, split_heads(grads_out), preferred_element_type=jnp.float32
        )
        extended_key_gradient = extended_key_gradient.at[first_row : stop_row + STRIDE].add(
            key_part.reshape(block_rows + STRIDE, width_local)
        )
        extended_value_gradient = extended_value_gradient.at[first_row : stop_row + STRIDE].add(
            value_part.reshape(block_rows + STRIDE, width_local)
        )
    halo_back = from_behind(
        jnp.stack([extended_key_gradient[:STRIDE], extended_value_gradient[:STRIDE]]).astype(
            jnp.bfloat16
        ),
        "seq",
        -1,
    ).astype(jnp.float32)
    band_dk = extended_key_gradient[STRIDE:].at[length - STRIDE :].add(halo_back[0])
    band_dv = extended_value_gradient[STRIDE:].at[length - STRIDE :].add(halo_back[1])
    query_grad = (query_parts[0] + returned[0]).astype(jnp.bfloat16)
    key_grad = (band_dk + returned[1]).astype(jnp.bfloat16)
    value_grad = (band_dv + returned[2]).astype(jnp.bfloat16)
    return (query_grad, key_grad, value_grad)


def solution(mesh):
    return jax.shard_map(
        per_device,
        mesh=mesh,
        in_specs=(P("seq", "head"), P("seq", "head"), P("seq", "head"), P(("seq", "head"), None)),
        out_specs=(P("seq", "head"), P("seq", "head"), P("seq", "head")),
        check_vma=False,
    )
```

profile of v0, /device:TPU:24, one launch (start us, length us, event | category | flops | bytes accessed | tf_op | source)
XLA Modules:
  0.0 235.0 jit_solution(18319919457815859158)
XLA Ops:
  0.6 1.7 copy.263
  2.4 4.8 %all-to-all-start = ((bf16[64,4,512]{2,0,1:T(8,128)(2,1)}), bf16[64,4,512]{2,0,1:T(8,128)(2,1)S(1)}, u32[]{:S(2)}, u32[]{:S(2)}) async-start(bf16[64,4,512]{2,0,1:T(8,128)(2,1)} %bitcast.113), calls=%async_computation | async-start | bytes 524288 | tf_op jit(solution)/shard_map/all_to_all | solution.py:53
  9.5 2.0 all-to-all-done
  11.8 1.8 copy.177
  13.6 12.9 %all-to-all-start.1 = ((bf16[4,1,256,512]{3,0,1,2:T(4,128)(2,1)}), bf16[4,1,256,512]{3,0,1,2:T(4,128)(2,1)S(1)}, u32[]{:S(2)}, u32[]{:S(2)}) async-start(bf16[4,1,256,512]{3,0,1,2:T(4,128)(2,1)} %copy.177), calls=%async_computation.1 | async-start | bytes 2097152 | tf_op jit(solution)/shard_map/all_to_all | solution.py:66
  27.4 3.4 %collective-permute-start = (bf16[2,256,512]{1,2,0:T(8,128)(2,1)}, bf16[2,256,512]{1,2,0:T(8,128)(2,1)S(1)}, u32[]{:S(2)}, u32[]{:S(2)}) collective-permute-start(bf16[2,256,512]{1,2,0:T(8,128)(2,1)} %pad_maximum_fusion.1), channel_id=1, source_target_pairs={{0,4},{4,8},{8,12},{12,16},{16,20},{20,24},{24,28},{28,32},{32,36}... | collective-permute-start | bytes 1572872 | tf_op jit(solution)/shard_map/ppermute | solution.py:18
  33.7 26.8 %collective-permute-done = bf16[2,256,512]{1,2,0:T(8,128)(2,1)S(1)} collective-permute-done((bf16[2,256,512]{1,2,0:T(8,128)(2,1)}, bf16[2,256,512]{1,2,0:T(8,128)(2,1)S(1)}, u32[]{:S(2)}, u32[]{:S(2)}) %collective-permute-start) | collective-permute-done | bytes 524320 | tf_op jit(solution)/shard_map/ppermute | solution.py:18
  62.0 1.5 fusion.55
  63.5 6.5 %slice_reduce_fusion.1 = (bf16[256,512]{1,0:T(8,128)(2,1)}, bf16[256,512]{1,0:T(8,128)(2,1)}, bf16[256,512]{1,0:T(8,128)(2,1)}, bf16[256,512]{1,0:T(8,128)(2,1)}) fusion(bf16[4,1,256,512]{3,0,1,2:T(4,128)(2,1)S(1)} %all-to-all-done.1), kind=kLoop, calls=%fused_computation.41 | loop fusion | bytes 2097152 | tf_op jit(solution)/shard_map/slice | solution.py:69
  71.1 1.8 reshape_squeeze.12
  72.9 1.9 fusion.54
  74.8 1.5 copy.180
  76.3 11.9 %all-to-all-start.2 = ((f32[4,64,4]{2,0,1:T(4,128)}), f32[4,64,4]{2,0,1:T(4,128)}, u32[]{:S(2)}, u32[]{:S(2)}) async-start(f32[4,64,4]{2,0,1:T(4,128)} %copy.180), calls=%async_computation.2 | async-start | bytes 262144 | tf_op jit(solution)/shard_map/all_to_all | solution.py:95
  88.2 1.4 select_reduce_fusion.1
  89.6 1.5 copy.182
  91.1 6.9 %all-to-all-done.2 = f32[4,64,4]{2,0,1:T(4,128)} async-done(((f32[4,64,4]{2,0,1:T(4,128)}), f32[4,64,4]{2,0,1:T(4,128)}, u32[]{:S(2)}, u32[]{:S(2)}) %all-to-all-start.2) | async-done | bytes 4128 | tf_op jit(solution)/shard_map/all_to_all | solution.py:95
  98.0 6.0 %all-to-all-start.3 = ((f32[4,64,4]{2,0,1:T(4,128)}), f32[4,64,4]{2,0,1:T(4,128)}, u32[]{:S(2)}, u32[]{:S(2)}) async-start(f32[4,64,4]{2,0,1:T(4,128)} %copy.182), calls=%async_computation.3 | async-start | bytes 262144 | tf_op jit(solution)/shard_map/all_to_all | solution.py:96
  105.4 1.8 reshape_squeeze.14
  107.2 1.6 copy.181
  108.7 1.6 all_to_all.38
  110.3 1.6 all_to_all.81
  112.0 2.0 all-to-all-done.3
  113.9 1.6 copy.183
  115.5 1.6 all_to_all.80
  117.1 1.6 all_to_all.82
  118.7 1.3 fusion.41
  120.0 1.5 copy.190
  121.5 9.5 %all-to-all-start.4 = ((f32[4,1,256]{0,1,2:T(1,128)}), f32[4,1,256]{0,1,2:T(1,128)}, u32[]{:S(2)}, u32[]{:S(2)}) async-start(f32[4,1,256]{0,1,2:T(1,128)} %copy.190), calls=%async_computation.4 | async-start | bytes 262144 | tf_op jit(solution)/shard_map/all_to_all | solution.py:99
  132.4 8.5 %all-to-all-done.4 = f32[4,1,256]{0,1,2:T(1,128)} async-done(((f32[4,1,256]{0,1,2:T(1,128)}), f32[4,1,256]{0,1,2:T(1,128)}, u32[]{:S(2)}, u32[]{:S(2)}) %all-to-all-start.4) | async-done | bytes 4128 | tf_op jit(solution)/shard_map/all_to_all | solution.py:99
  141.8 2.7 %multiply_reduce_fusion = (f32[4,64,4]{1,2,0:T(4,128)}, f32[4,64,4,64]{1,3,2,0:T(8,128)}) fusion(f32[4,64,4,64]{1,3,2,0:T(8,128)S(1)} %get-tuple-element.97, f32[4,64,4]{1,2,0:T(4,128)S(1)} %copy.192, pred[64,64]{0,1:T(8,128)(4,1)S(1)} %iota_compare_fusion.2, bf16[64,4,4,128]{3,2,1,0:T(4,128)(2,1)S(1)} %reshape_squeeze.15, ...), kind=kOutput, calls=%fused_computation.53 | convolution fusion | flops 17038336 | bytes 1060864 | tf_op jit(solution)/shard_map/prhd,qrhd->hprq/dot_general | solution.py:123
  144.5 1.5 copy.195
  145.9 6.3 %all-to-all-start.5 = ((f32[4,64,4]{2,0,1:T(4,128)}), f32[4,64,4]{2,0,1:T(4,128)}, u32[]{:S(2)}, u32[]{:S(2)}) async-start(f32[4,64,4]{2,0,1:T(4,128)} %copy.195), calls=%async_computation.5 | async-start | bytes 262144 | tf_op jit(solution)/shard_map/all_to_all | solution.py:127
  152.2 3.5 %fusion = (f32[4,256]{1,0:T(4,128)}, f32[4,512,256]{2,1,0:T(8,128)}) fusion(f32[4,256,512]{1,2,0:T(8,128)S(1)} %get-tuple-element.99, f32[4,256]{1,0:T(4,128)} %log_add_fusion, pred[256,512]{0,1:T(8,128)(4,1)S(1)} %fusion.27, bf16[256,4,128]{0,2,1:T(8,128)(2,1)S(1)} %copy-done.2, bf16[256,4,128]{2,0,1:T(8,128)(2,1)} %copy.186, bf16[256,4,128]{2,0,1:T(8,128)(2,1)} %copy.185), kind=kOutput, calls=%fused_computation.2 | convolution fusion | flops 137362432 | bytes 5120000 | tf_op jit(solution)/shard_map/qhd,khd->hqk/dot_general | solution.py:109
  155.7 6.4 %all-to-all-done.5 = f32[4,64,4]{2,0,1:T(4,128)} async-done(((f32[4,64,4]{2,0,1:T(4,128)}), f32[4,64,4]{2,0,1:T(4,128)}, u32[]{:S(2)}, u32[]{:S(2)}) %all-to-all-start.5) | async-done | bytes 4128 | tf_op jit(solution)/shard_map/all_to_all | solution.py:127
  162.1 1.6 copy.196
  163.7 1.6 all_to_all.86
  166.6 1.5 copy.200
  168.1 16.0 %all_to_all.97 = f32[4,1,256]{0,1,2:T(1,128)} all-to-all(f32[4,1,256]{0,1,2:T(1,128)} %copy.200), channel_id=1, replica_groups=mesh['seq'=64,'head'=4] {'seq'}, dimensions={2} | all-to-all | bytes 8192 | tf_op jit(solution)/shard_map/all_to_all | solution.py:129
  184.1 1.6 copy.202
  187.0 1.9 fusion.9
  194.6 1.5 copy.212
  196.1 6.1 %all-to-all-start.7 = ((bf16[3,64,4,512]{3,2,0,1:T(4,128)(2,1)}), bf16[3,64,4,512]{3,2,0,1:T(4,128)(2,1)}, u32[]{:S(2)}, u32[]{:S(2)}) async-start(bf16[3,64,4,512]{3,2,0,1:T(4,128)(2,1)} %copy.212), calls=%async_computation.7 | async-start | bytes 1572864 | tf_op jit(solution)/shard_map/all_to_all | solution.py:148
  204.8 2.1 fusion.2
  208.7 2.7 %collective-permute-start.1 = (bf16[2,256,512]{2,1,0:T(8,128)(2,1)}, bf16[2,256,512]{2,1,0:T(8,128)(2,1)}, u32[]{:S(2)}, u32[]{:S(2)}) collective-permute-start(bf16[2,256,512]{2,1,0:T(8,128)(2,1)} %pad_maximum_fusion.3), channel_id=1, source_target_pairs={{4,0},{8,4},{12,8},{16,12},{20,16},{24,20},{28,24},{32,28},{36,32}... | collective-permute-start | bytes 1572872 | tf_op jit(solution)/shard_map/ppermute | solution.py:18
  211.6 1.4 convolution_multiply_fusion.1
  214.2 12.1 %collective-permute-done.1 = bf16[2,256,512]{2,1,0:T(8,128)(2,1)} collective-permute-done((bf16[2,256,512]{2,1,0:T(8,128)(2,1)}, bf16[2,256,512]{2,1,0:T(8,128)(2,1)}, u32[]{:S(2)}, u32[]{:S(2)}) %collective-permute-start.1) | collective-permute-done | bytes 524320 | tf_op jit(solution)/shard_map/ppermute | solution.py:18
  227.5 2.2 fusion.52
  232.0 2.0 add_convert_fusion
  (82 shorter events, 31.1 us)
Async XLA Ops:
  0.6 8.7 %copy-start.8 = (bf16[256,512]{1,0:T(8,128)(2,1)S(1)}, bf16[256,512]{1,0:T(8,128)(2,1)}, u32[]{:S(2)}) copy-start(bf16[256,512]{1,0:T(8,128)(2,1)} %param.22) | copy-start | bytes 786436
  2.4 9.2 %all-to-all-start = ((bf16[64,4,512]{2,0,1:T(8,128)(2,1)}), bf16[64,4,512]{2,0,1:T(8,128)(2,1)S(1)}, u32[]{:S(2)}, u32[]{:S(2)}) async-start(bf16[64,4,512]{2,0,1:T(8,128)(2,1)} %bitcast.113), calls=%async_computation | async-start | bytes 524288 | tf_op jit(solution)/shard_map/all_to_all | solution.py:53
  13.6 49.9 %all-to-all-start.1 = ((bf16[4,1,256,512]{3,0,1,2:T(4,128)(2,1)}), bf16[4,1,256,512]{3,0,1,2:T(4,128)(2,1)S(1)}, u32[]{:S(2)}, u32[]{:S(2)}) async-start(bf16[4,1,256,512]{3,0,1,2:T(4,128)(2,1)} %copy.177), calls=%async_computation.1 | async-start | bytes 2097152 | tf_op jit(solution)/shard_map/all_to_all | solution.py:66
  27.4 33.0 %collective-permute-start = (bf16[2,256,512]{1,2,0:T(8,128)(2,1)}, bf16[2,256,512]{1,2,0:T(8,128)(2,1)S(1)}, u32[]{:S(2)}, u32[]{:S(2)}) collective-permute-start(bf16[2,256,512]{1,2,0:T(8,128)(2,1)} %pad_maximum_fusion.1), channel_id=1, source_target_pairs={{0,4},{4,8},{8,12},{12,16},{16,20},{20,24},{24,28},{28,32},{32,36}... | collective-permute-start | bytes 1572872 | tf_op jit(solution)/shard_map/ppermute | solution.py:18
  71.1 1.8 copy-start.9
  72.9 31.5 %copy-start.5 = (bf16[1,256,512]{1,2,0:T(8,128)(2,1)S(1)}, bf16[1,256,512]{1,2,0:T(8,128)(2,1)}, u32[]{:S(2)}) copy-start(bf16[1,256,512]{1,2,0:T(8,128)(2,1)} %get-tuple-element.95) | copy-start | bytes 786436
  74.8 30.5 %copy-start.4 = (bf16[256,512]{1,0:T(8,128)(2,1)S(1)}, bf16[256,512]{1,0:T(8,128)(2,1)}, u32[]{:S(2)}) copy-start(bf16[256,512]{1,0:T(8,128)(2,1)} %get-tuple-element.84) | copy-start | bytes 786436
  76.3 21.7 %all-to-all-start.2 = ((f32[4,64,4]{2,0,1:T(4,128)}), f32[4,64,4]{2,0,1:T(4,128)}, u32[]{:S(2)}, u32[]{:S(2)}) async-start(f32[4,64,4]{2,0,1:T(4,128)} %copy.180), calls=%async_computation.2 | async-start | bytes 262144 | tf_op jit(solution)/shard_map/all_to_all | solution.py:95
  98.0 15.9 %all-to-all-start.3 = ((f32[4,64,4]{2,0,1:T(4,128)}), f32[4,64,4]{2,0,1:T(4,128)}, u32[]{:S(2)}, u32[]{:S(2)}) async-start(f32[4,64,4]{2,0,1:T(4,128)} %copy.182), calls=%async_computation.3 | async-start | bytes 262144 | tf_op jit(solution)/shard_map/all_to_all | solution.py:96
  105.4 46.9 %copy-start.2 = (bf16[256,4,128]{0,2,1:T(8,128)(2,1)S(1)}, bf16[256,4,128]{0,2,1:T(8,128)(2,1)}, u32[]{:S(2)}) copy-start(bf16[256,4,128]{0,2,1:T(8,128)(2,1)} %copy.217) | copy-start | bytes 786436
  121.5 19.3 %all-to-all-start.4 = ((f32[4,1,256]{0,1,2:T(1,128)}), f32[4,1,256]{0,1,2:T(1,128)}, u32[]{:S(2)}, u32[]{:S(2)}) async-start(f32[4,1,256]{0,1,2:T(1,128)} %copy.190), calls=%async_computation.4 | async-start | bytes 262144 | tf_op jit(solution)/shard_map/all_to_all | solution.py:99
  145.9 16.2 %all-to-all-start.5 = ((f32[4,64,4]{2,0,1:T(4,128)}), f32[4,64,4]{2,0,1:T(4,128)}, u32[]{:S(2)}, u32[]{:S(2)}) async-start(f32[4,64,4]{2,0,1:T(4,128)} %copy.195), calls=%async_computation.5 | async-start | bytes 262144 | tf_op jit(solution)/shard_map/all_to_all | solution.py:127
  185.7 3.1 %copy-start.10 = (bf16[64,4,4,128]{3,2,1,0:T(4,128)(2,1)S(1)}, bf16[64,4,4,128]{3,2,1,0:T(4,128)(2,1)}, u32[]{:S(2)}) copy-start(bf16[64,4,4,128]{3,2,1,0:T(4,128)(2,1)} %reshape_squeeze.12) | copy-start | bytes 786436
  193.6 8.6 %copy-start.11 = (f32[4,256]{1,0:T(4,128)S(1)}, f32[4,256]{1,0:T(4,128)}, u32[]{:S(2)}) copy-start(f32[4,256]{1,0:T(4,128)} %log_add_fusion) | copy-start | bytes 12292
  196.1 31.3 %all-to-all-start.7 = ((bf16[3,64,4,512]{3,2,0,1:T(4,128)(2,1)}), bf16[3,64,4,512]{3,2,0,1:T(4,128)(2,1)}, u32[]{:S(2)}, u32[]{:S(2)}) async-start(bf16[3,64,4,512]{3,2,0,1:T(4,128)(2,1)} %copy.212), calls=%async_computation.7 | async-start | bytes 1572864 | tf_op jit(solution)/shard_map/all_to_all | solution.py:148
  202.2 2.4 %copy-start.3 = (f32[4,64,4]{2,1,0:T(8,128)S(1)}, f32[4,64,4]{2,1,0:T(8,128)}, u32[]{:S(2)}) copy-start(f32[4,64,4]{2,1,0:T(8,128)} %copy.196) | copy-start | bytes 12292
  202.2 2.5 %copy-start.12 = (f32[4,256]{1,0:T(4,128)S(1)}, f32[4,256]{1,0:T(4,128)}, u32[]{:S(2)}) copy-start(f32[4,256]{1,0:T(4,128)} %get-tuple-element.100) | copy-start | bytes 12292
  202.8 1.0 copy-start.1
  206.9 1.0 copy-start.6
  207.4 4.2 %copy-start = (f32[512,4,128]{0,2,1:T(8,128)}, f32[512,4,128]{0,2,1:T(8,128)S(1)}, u32[]{:S(2)}) copy-start(f32[512,4,128]{0,2,1:T(8,128)S(1)} %fusion.3) | copy-start | bytes 3145732
  207.4 4.0 %slice-start.1 = ((f32[512,4,128]{0,2,1:T(8,128)}), f32[256,4,128]{0,2,1:T(8,128)S(1)}, s32[]{:S(2)}) async-start(f32[512,4,128]{0,2,1:T(8,128)} %copy-done.1), calls=%async_computation.9 | async-start | bytes 1048576 | tf_op jit(solution)/shard_map/slice | solution.py:198
  208.7 2.9 %copy-start.7 = (bf16[256,4,128]{2,0,1:T(8,128)(2,1)S(1)}, bf16[256,4,128]{2,0,1:T(8,128)(2,1)}, u32[]{:S(2)}) copy-start(bf16[256,4,128]{2,0,1:T(8,128)(2,1)} %copy.172) | copy-start | bytes 786436
  208.7 17.6 %collective-permute-start.1 = (bf16[2,256,512]{2,1,0:T(8,128)(2,1)}, bf16[2,256,512]{2,1,0:T(8,128)(2,1)}, u32[]{:S(2)}, u32[]{:S(2)}) collective-permute-start(bf16[2,256,512]{2,1,0:T(8,128)(2,1)} %pad_maximum_fusion.3), channel_id=1, source_target_pairs={{4,0},{8,4},{12,8},{16,12},{20,16},{24,20},{28,24},{32,28},{36,32}... | collective-permute-start | bytes 1572872 | tf_op jit(solution)/shard_map/ppermute | solution.py:18
  211.6 2.4 %slice-start = ((f32[512,4,128]{0,2,1:T(8,128)}), f32[256,4,128]{0,2,1:T(8,128)S(1)}, s32[]{:S(2)}) async-start(f32[512,4,128]{0,2,1:T(8,128)} %copy-done), calls=%async_computation.8 | async-start | bytes 1048576 | tf_op jit(solution)/shard_map/slice | solution.py:197
where the time goes:
time: 238 us; the launch traced here: 235 us
  waiting for transfers between devices  64.7 us (27%)
  starting transfers between devices  63.6 us (27%)
  local copies, waits for them, and re-layouts  58.4 us (25%)
  other arithmetic  16.3 us (7%)
  blocking collectives  16 us (7%)
  matrix products  14.9 us (6%)
    ppermute x2, waiting for transfers between devices, from_behind(): lax.ppermute(value, axis, [(source, source + steps) for source in range(i...  38.9 us
    all_to_all x1, blocking collectives, per_device(): lax.all_to_all(delta_home, 'seq', split_axis=2, concat_axis=1, tiled=True)  16 us
    all_to_all x1, starting transfers between devices, per_device(): lax.all_to_all(stacked, 'seq', split_axis=2, concat_axis=1, tiled=True)  12.9 us
    all_to_all x1, starting transfers between devices, per_device(): lax.all_to_all(class_max, 'seq', split_axis=1, concat_axis=2, tiled=True)  11.9 us
    all_to_all x1, starting transfers between devices, per_device(): lax.all_to_all(lse_home, 'seq', split_axis=2, concat_axis=1, tiled=True)  9.54 us
    all_to_all x1, waiting for transfers between devices, per_device(): lax.all_to_all(lse_home, 'seq', split_axis=2, concat_axis=1, tiled=True)  8.48 us
    all_to_all x1, waiting for transfers between devices, per_device(): lax.all_to_all(class_max, 'seq', split_axis=1, concat_axis=2, tiled=True)  6.91 us
    slice x1, local copies, waits for them, and re-layouts, per_device(): class_v = split_heads(classes[2])  6.54 us
  transfers between devices with their start and end apart: 9, of which 7 were waited for; matrix products, arithmetic and copies ran while one was open for 13% of the time, Pallas kernels for 0%

commit v1 on v0

v1 whole, which is shorter than its diff:
```python
import functools

import jax
import jax.numpy as jnp
from jax import lax
from jax.experimental import pallas as pl
from jax.experimental.pallas import tpu as pltpu
from jax.sharding import PartitionSpec as P

HEAD_DIM = 128
STRIDE = 256
TILE = 16
NEG_LARGE = -1e30
SCALE = HEAD_DIM**-0.5
MESH = pl.DeviceIdType.MESH
F32 = jnp.float32
BF16 = jnp.bfloat16


def dot_nt(a, b):
    return lax.dot_general(a, b, (((1,), (1,)), ((), ())), preferred_element_type=F32)


def dot_nn(a, b):
    return lax.dot_general(a, b, (((1,), (0,)), ((), ())), preferred_element_type=F32)


def dot_tn(a, b):
    return lax.dot_general(a, b, (((0,), (0,)), ((), ())), preferred_element_type=F32)


def iota(shape, axis):
    return lax.broadcasted_iota(jnp.int32, shape, axis)


def kernel(
    seq_count, head_count,
    q_ref, k_ref, v_ref, og_ref,
    dq_ref, dk_ref, dv_ref,
    g_home, halo, back_snd, back_rcv,
    snd, rcv, gsnd, grcv, stat_snd, stat_rcv, cstat_snd, cstat_rcv, grad_snd, grad_rcv,
    wide, classes, gwide, e_diag, e_prev, pg_diag, pg_prev, stat_col, acc,
    g_send_sem, g_recv_sem, halo_send_sem, halo_recv_sem, back_send_sem, back_recv_sem,
    send_sem, recv_sem,
):
    s = lax.axis_index("seq")
    hd = lax.axis_index("head")
    others = seq_count - 1
    heads = q_ref.shape[1] // HEAD_DIM
    tiles = STRIDE // TILE
    width = q_ref.shape[1]
    after = lax.rem(s + 1, seq_count)
    before = lax.rem(s + seq_count - 1, seq_count)
    part = og_ref.shape[0]

    barrier = pltpu.get_barrier_semaphore()

    @pl.loop(1, seq_count)
    def _(i):
        pl.semaphore_signal(
            barrier, inc=1, device_id=(lax.rem(s + i, seq_count), hd), device_id_type=MESH
        )

    @pl.loop(1, head_count)
    def _(i):
        pl.semaphore_signal(
            barrier, inc=1, device_id=(s, lax.rem(hd + i, head_count)), device_id_type=MESH
        )

    for j, ref in enumerate((q_ref, k_ref, v_ref)):
        for h in range(heads):
            snd[h * tiles : (h + 1) * tiles, j] = ref[
                :, h * HEAD_DIM : (h + 1) * HEAD_DIM
            ].reshape(tiles, TILE, HEAD_DIM)
    own_rows = pl.ds(pl.multiple_of(hd * part, part), part)
    g_home[own_rows, :] = og_ref[:, pl.ds(pl.multiple_of(hd * width, width), width)]

    pl.semaphore_wait(barrier, others + head_count - 1)

    def send_all(src, dst, index):
        @pl.loop(1, seq_count)
        def _(i):
            peer = lax.rem(s + i, seq_count)
            pltpu.make_async_remote_copy(
                src_ref=src.at[peer],
                dst_ref=dst.at[s],
                send_sem=send_sem.at[index],
                recv_sem=recv_sem.at[index],
                device_id=(peer, hd),
                device_id_type=MESH,
            ).start()

    def whole(src, dst, index):
        return pltpu.make_async_remote_copy(
            src_ref=src.at[pl.ds(0, others)],
            dst_ref=dst.at[pl.ds(0, others)],
            send_sem=send_sem.at[index],
            recv_sem=recv_sem.at[index],
            device_id=(after, hd),
            device_id_type=MESH,
        )

    g_copies = []
    for i in range(1, head_count):
        peer = lax.rem(hd + i, head_count)
        copy = pltpu.make_async_remote_copy(
            src_ref=og_ref.at[:, pl.ds(pl.multiple_of(peer * width, width), width)],
            dst_ref=g_home.at[own_rows, :],
            send_sem=g_send_sem.at[i],
            recv_sem=g_recv_sem.at[i],
            device_id=(s, peer),
            device_id_type=MESH,
        )
        copy.start()
        g_copies.append(copy)
    halo_copies = []
    for j, ref in enumerate((k_ref, v_ref)):
        copy = pltpu.make_async_remote_copy(
            src_ref=ref,
            dst_ref=halo.at[j],
            send_sem=halo_send_sem.at[j],
            recv_sem=halo_recv_sem.at[j],
            device_id=(after, hd),
            device_id_type=MESH,
        )
        copy.start()
        halo_copies.append(copy)
    send_all(snd, rcv, 0)
    rcv[s] = snd[s]

    for copy in g_copies:
        copy.wait_recv()
    for h in range(heads):
        gsnd[h * tiles : (h + 1) * tiles] = g_home[
            :, h * HEAD_DIM : (h + 1) * HEAD_DIM
        ].reshape(tiles, TILE, HEAD_DIM)
    send_all(gsnd, grcv, 1)
    grcv[s] = gsnd[s]

    for copy in halo_copies:
        copy.wait_recv()

    row = iota((STRIDE, STRIDE), 0)
    col = iota((STRIDE, STRIDE), 1)
    lane = iota((STRIDE, HEAD_DIM), 1)
    row_in_tile = lax.rem(iota((STRIDE, HEAD_DIM), 0), TILE)

    @pl.loop(0, heads)
    def _(h):
        at = pl.ds(pl.multiple_of(h * HEAD_DIM, HEAD_DIM), HEAD_DIM)
        qh, gh = q_ref[:, at], g_home[:, at]
        sd = jnp.where(col <= row, dot_nt(qh, k_ref[:, at]) * SCALE, NEG_LARGE)
        sp = jnp.where((col > row) & (s > 0), dot_nt(qh, halo[0, :, at]) * SCALE, NEG_LARGE)
        top = jnp.maximum(
            jnp.max(sd, axis=1, keepdims=True), jnp.max(sp, axis=1, keepdims=True)
        )
        ed, ep = jnp.exp(sd - top), jnp.exp(sp - top)
        gd, gp = dot_nt(gh, v_ref[:, at]), dot_nt(gh, halo[1, :, at])
        total = jnp.sum(ed, axis=1, keepdims=True) + jnp.sum(ep, axis=1, keepdims=True)
        weighted = jnp.sum(ed * gd, axis=1, keepdims=True) + jnp.sum(
            ep * gp, axis=1, keepdims=True
        )
        e_diag[h], e_prev[h], pg_diag[h], pg_prev[h] = ed, ep, gd, gp
        stat_col[h] = jnp.where(lane == 0, top, jnp.where(lane == 1, total, weighted))
        spread = jnp.where(
            lane == row_in_tile,
            top,
            jnp.where(
                lane == row_in_tile + TILE,
                total,
                jnp.where(lane == row_in_tile + 2 * TILE, weighted, 0.0),
            ),
        )
        stat_snd[pl.ds(pl.multiple_of(h * tiles, tiles), tiles), 0, :] = jnp.sum(
            spread.reshape(tiles, TILE, HEAD_DIM), axis=1
        )

    send_all(stat_snd, stat_rcv, 2)
    stat_rcv[s] = stat_snd[s]

    whole(snd, rcv, 0).wait_recv()
    whole(gsnd, grcv, 1).wait_recv()
    for j in range(4):
        block = rcv[:, j] if j < 3 else grcv[...]
        wide[j] = block.reshape(seq_count * TILE, HEAD_DIM).astype(F32)
    for j in range(4):
        for r in range(TILE):
            classes[j, r * seq_count : (r + 1) * seq_count, :] = wide[
                j, pl.ds(r, seq_count, stride=TILE), :
            ].astype(BF16)
    whole(stat_snd, stat_rcv, 2).wait_recv()
    band = stat_rcv[:, 0, :]

    pair = 2 * seq_count
    prow = iota((pair, pair), 0)
    pcol = iota((pair, pair), 1)
    allowed = ((prow < seq_count) == (pcol < seq_count)) & (pcol < prow)
    slane = iota((seq_count, HEAD_DIM), 1)
    stats = jnp.zeros((seq_count, HEAD_DIM), F32)
    for p in range(TILE // 2):
        rows = slice(p * pair, (p + 1) * pair)
        cq, ck, cv, cg = (classes[j, rows, :] for j in range(4))
        sc = jnp.where(allowed, dot_nt(cq, ck) * SCALE, NEG_LARGE)
        top = jnp.max(sc, axis=1, keepdims=True)
        ec = jnp.where(allowed, jnp.exp(sc - top), 0.0)
        pg = dot_nt(cg, cv)
        total = jnp.sum(ec, axis=1, keepdims=True)
        weighted = jnp.sum(ec * pg, axis=1, keepdims=True)
        for c in range(2):
            r = 2 * p + c
            half = slice(c * seq_count, (c + 1) * seq_count)
            for n, value in enumerate((top, total, weighted)):
                stats = jnp.where(slane == n * TILE + r, value[half], stats)
        b_top, b_total, b_weighted = (
            jnp.concatenate(
                [band[:, n * TILE + 2 * p + c : n * TILE + 2 * p + c + 1] for c in range(2)], axis=0
            )
            for n in range(3)
        )
        peak = jnp.maximum(top, b_top)
        f_class, f_band = jnp.exp(top - peak), jnp.exp(b_top - peak)
        inverse = 1.0 / (total * f_class + b_total * f_band)
        delta = (weighted * f_class + b_weighted * f_band) * inverse
        probs = ec * (f_class * inverse)
        sgrad = (probs * (pg - delta)).astype(BF16)
        grads = (
            dot_nn(sgrad, ck) * SCALE,
            dot_tn(sgrad, cq) * SCALE,
            dot_tn(probs.astype(BF16), cg),
        )
        for j in range(3):
            for c in range(2):
                gwide[j, pl.ds(2 * p + c, seq_count, stride=TILE), :] = grads[j][
                    c * seq_count : (c + 1) * seq_count
                ]
    cstat_snd[:, 0, :] = stats
    send_all(cstat_snd, cstat_rcv, 3)
    cstat_rcv[s] = cstat_snd[s]
    for j in range(3):
        grad_snd[:, j] = gwide[j].reshape(seq_count, TILE, HEAD_DIM).astype(BF16)
    send_all(grad_snd, grad_rcv, 4)
    grad_rcv[s] = grad_snd[s]

    whole(cstat_snd, cstat_rcv, 3).wait_recv()

    @pl.loop(0, heads)
    def _(h):
        at = pl.ds(pl.multiple_of(h * HEAD_DIM, HEAD_DIM), HEAD_DIM)
        got = cstat_rcv[pl.ds(pl.multiple_of(h * tiles, tiles), tiles), 0, :]
        got = jnp.broadcast_to(got[:, None, :], (tiles, TILE, HEAD_DIM)).reshape(
            STRIDE, HEAD_DIM
        )
        c_top, c_total, c_weighted = (
            jnp.sum(
                jnp.where(lane == row_in_tile + n * TILE, got, 0.0), axis=1, keepdims=True
            )
            for n in range(3)
        )
        own = stat_col[h]
        top, total, weighted = own[:, 0:1], own[:, 1:2], own[:, 2:3]
        peak = jnp.maximum(top, c_top)
        f_class, f_band = jnp.exp(c_top - peak), jnp.exp(top - peak)
        inverse = 1.0 / (c_total * f_class + total * f_band)
        delta = (c_weighted * f_class + weighted * f_band) * inverse
        factor = f_band * inverse
        pd, pp = e_diag[h] * factor, e_prev[h] * factor
        sd = (pd * (pg_diag[h] - delta)).astype(BF16)
        sp = (pp * (pg_prev[h] - delta)).astype(BF16)
        qh, gh = q_ref[:, at], g_home[:, at]
        back_snd[0, :, at] = (dot_tn(sp, qh) * SCALE).astype(BF16)
        back_snd[1, :, at] = dot_tn(pp.astype(BF16), gh).astype(BF16)
        acc[0, :, at] = (dot_nn(sd, k_ref[:, at]) + dot_nn(sp, halo[0, :, at])) * SCALE
        acc[1, :, at] = dot_tn(sd, qh) * SCALE
        acc[2, :, at] = dot_tn(pd.astype(BF16), gh)

    back = pltpu.make_async_remote_copy(
        src_ref=back_snd,
        dst_ref=back_rcv,
        send_sem=back_send_sem,
        recv_sem=back_recv_sem,
        device_id=(before, hd),
        device_id_type=MESH,
    )
    back.start()
    whole(grad_snd, grad_rcv, 4).wait_recv()
    back.wait_recv()
    for h in range(heads):
        at = slice(h * HEAD_DIM, (h + 1) * HEAD_DIM)
        for j, out in enumerate((dq_ref, dk_ref, dv_ref)):
            value = acc[j, :, at] + grad_rcv[h * tiles : (h + 1) * tiles, j].reshape(
                STRIDE, HEAD_DIM
            ).astype(F32)
            if j > 0:
                value = value + back_rcv[j - 1, :, at].astype(F32)
            out[:, at] = value.astype(BF16)

    for copy in g_copies + halo_copies:
        copy.wait_send()
    for index, buffers in enumerate(
        ((snd, rcv), (gsnd, grcv), (stat_snd, stat_rcv), (cstat_snd, cstat_rcv), (grad_snd, grad_rcv))
    ):
        whole(*buffers, index).wait_send()
    back.wait_send()


def per_device(queries, keys, values, out_grad):
    length, width = queries.shape
    seq_count = lax.axis_size("seq")
    head_count = lax.axis_size("head")
    heads = width // HEAD_DIM
    assert length == STRIDE and seq_count * TILE == STRIDE * heads
    vmem = pl.BlockSpec(memory_space=pltpu.VMEM)
    tile = (TILE, HEAD_DIM)
    return pl.pallas_call(
        functools.partial(kernel, seq_count, head_count),
        out_shape=[jax.ShapeDtypeStruct(queries.shape, BF16)] * 3,
        in_specs=[vmem] * 4,
        out_specs=[vmem] * 3,
        scratch_shapes=[
            pltpu.VMEM((length, width), BF16),
            pltpu.VMEM((2, length, width), BF16),
            pltpu.VMEM((2, length, width), BF16),
            pltpu.VMEM((2, length, width), BF16),
            pltpu.VMEM((seq_count, 3) + tile, BF16),
            pltpu.VMEM((seq_count, 3) + tile, BF16),
            pltpu.VMEM((seq_count,) + tile, BF16),
            pltpu.VMEM((seq_count,) + tile, BF16),
            pltpu.VMEM((seq_count, 1, HEAD_DIM), F32),
            pltpu.VMEM((seq_count, 1, HEAD_DIM), F32),
            pltpu.VMEM((seq_count, 1, HEAD_DIM), F32),
            pltpu.VMEM((seq_count, 1, HEAD_DIM), F32),
            pltpu.VMEM((seq_count, 3) + tile, BF16),
            pltpu.VMEM((seq_count, 3) + tile, BF16),
            pltpu.VMEM((4, seq_count * TILE, HEAD_DIM), F32),
            pltpu.VMEM((4, seq_count * TILE, HEAD_DIM), BF16),
            pltpu.VMEM((3, seq_count * TILE, HEAD_DIM), F32),
            pltpu.VMEM((heads, STRIDE, STRIDE), F32),
            pltpu.VMEM((heads, STRIDE, STRIDE), F32),
            pltpu.VMEM((heads, STRIDE, STRIDE), F32),
            pltpu.VMEM((heads, STRIDE, STRIDE), F32),
            pltpu.VMEM((heads, STRIDE, HEAD_DIM), F32),
            pltpu.VMEM((3, length, width), F32),
            pltpu.SemaphoreType.DMA((head_count,)),
            pltpu.SemaphoreType.DMA((head_count,)),
            pltpu.SemaphoreType.DMA((2,)),
            pltpu.SemaphoreType.DMA((2,)),
            pltpu.SemaphoreType.DMA,
            pltpu.SemaphoreType.DMA,
            pltpu.SemaphoreType.DMA((5,)),
            pltpu.SemaphoreType.DMA((5,)),
        ],
        compiler_params=pltpu.CompilerParams(
            collective_id=0, has_side_effects=True, vmem_limit_bytes=48 * 2**20
        ),
    )(queries, keys, values, out_grad)


def solution(mesh):
    return jax.shard_map(
        per_device,
        mesh=mesh,
        in_specs=(P("seq", "head"), P("seq", "head"), P("seq", "head"), P(("seq", "head"), None)),
        out_specs=(P("seq", "head"), P("seq", "head"), P("seq", "head")),
        check_vma=False,
    )
```

time: 238 us -> 95.8 us (0.40)
  Pallas kernels: 0 us -> 87.7 us
  waiting for transfers between devices: 64.7 us -> 0 us
  starting transfers between devices: 63.6 us -> 0 us
  local copies, waits for them, and re-layouts: 58.4 us -> 5.9 us
  other arithmetic: 16.3 us -> 0 us
  blocking collectives: 16 us -> 0 us
  matrix products: 14.9 us -> 0 us
    pallas_call x0 -> x1, Pallas kernels: none -> 87.7 us  [per_device(): pl.pallas_call(functools.partial(kernel, seq_count, head_count), out_shap...]
    all_to_all x7 -> x0, starting transfers between devices: 57.6 us -> none  [the longest x1 12.9 us: per_device(): lax.all_to_all(stacked, 'seq', split_axis=2, concat_axis=1, tiled=True)]
    ppermute x2 -> x0, waiting for transfers between devices: 38.9 us -> none  [from_behind(): lax.ppermute(value, axis, [(source, source + steps) for source in range(i...]
    all_to_all x7 -> x0, waiting for transfers between devices: 25.8 us -> none  [the longest x1 8.48 us: per_device(): lax.all_to_all(lse_home, 'seq', split_axis=2, concat_axis=1, tiled=True)]
    all_to_all x1 -> x0, blocking collectives: 16 us -> none  [per_device(): lax.all_to_all(delta_home, 'seq', split_axis=2, concat_axis=1, tiled=True)]
    dot_general x10 -> x0, matrix products: 14.9 us -> none  [the longest x1 3.46 us: band_terms(): jnp.einsum('qhd,khd->hqk', split_heads(grads_out), split_heads(ext_values...]
    all_to_all x10 -> x0, local copies, waits for them, and re-layouts: 14.6 us -> none  [the longest x3 4.8 us: per_device(): lax.all_to_all(class_max, 'seq', split_axis=1, concat_axis=2, tiled=True)]
    slice x11 -> x0, local copies, waits for them, and re-layouts: 9.92 us -> none  [the longest x1 6.54 us: per_device(): class_v = split_heads(classes[2])]
  transfers between devices with their start and end apart: 9 -> 0, of which waited for: 7 -> 0; matrix products, arithmetic and copies ran while one was open for 13% -> 0% of each run, Pallas kernels for 0% -> 0%
where the time goes in v1:
time: 95.8 us; the launch traced here: 94.3 us
  Pallas kernels  87.7 us (92%)
  local copies, waits for them, and re-layouts  5.9 us (6%)
    pallas_call x1, Pallas kernels, per_device(): pl.pallas_call(functools.partial(kernel, seq_count, head_count), out_shap...  87.7 us
    unnamed x11, local copies, waits for them, and re-layouts  5.9 us

profile of v1, /device:TPU:24, one launch (start us, length us, event | category | flops | bytes accessed | tf_op | source)
XLA Modules:
  0.0 94.3 jit_solution(2391950629016184667)
XLA Ops:
  0.6 0.0 copy-start
  0.6 0.9 copy-done
  1.6 0.0 copy-start.1
  1.6 0.9 %copy-done.1 = bf16[256,512]{1,0:T(8,128)(2,1)S(1)} copy-done((bf16[256,512]{1,0:T(8,128)(2,1)S(1)}, bf16[256,512]{1,0:T(8,128)(2,1)}, u32[]{:S(2)}) %copy-start.1) | copy-done | bytes 262168
  2.5 0.0 copy-start.2
  2.5 0.9 %copy-done.2 = bf16[256,512]{1,0:T(8,128)(2,1)S(1)} copy-done((bf16[256,512]{1,0:T(8,128)(2,1)S(1)}, bf16[256,512]{1,0:T(8,128)(2,1)}, u32[]{:S(2)}) %copy-start.2) | copy-done | bytes 262168
  3.5 0.0 copy-start.3
  3.5 0.9 %copy-done.3 = bf16[64,2048]{1,0:T(8,128)(2,1)S(1)} copy-done((bf16[64,2048]{1,0:T(8,128)(2,1)S(1)}, bf16[64,2048]{1,0:T(8,128)(2,1)}, u32[]{:S(2)}) %copy-start.3) | copy-done | bytes 262168
  4.4 87.7 %shard_map.67 = (bf16[256,512]{1,0:T(8,128)(2,1)S(1)}, bf16[256,512]{1,0:T(8,128)(2,1)S(1)}, bf16[256,512]{1,0:T(8,128)(2,1)S(1)}) custom-call(bf16[256,512]{1,0:T(8,128)(2,1)S(1)} %copy-done, bf16[256,512]{1,0:T(8,128)(2,1)S(1)} %copy-done.1, bf16[256,512]{1,0:T(8,128)(2,1)S(1)} %copy-done.2, bf16[64,2048]{1,0:T(8,128)(2,1)S(1)} %copy-done.3), custom_call_target="tpu_custom_call" | custom-call | tf_op jit(solution)/shard_map/pallas_call | solution.py:314
  92.2 0.7 copy.10
  92.9 0.7 copy.11
  93.6 0.7 copy.12
Async XLA Ops:
  0.6 1.0 %copy-start = (bf16[256,512]{1,0:T(8,128)(2,1)S(1)}, bf16[256,512]{1,0:T(8,128)(2,1)}, u32[]{:S(2)}) copy-start(bf16[256,512]{1,0:T(8,128)(2,1)} %q_ref.1) | copy-start | bytes 786436
  1.6 0.9 %copy-start.1 = (bf16[256,512]{1,0:T(8,128)(2,1)S(1)}, bf16[256,512]{1,0:T(8,128)(2,1)}, u32[]{:S(2)}) copy-start(bf16[256,512]{1,0:T(8,128)(2,1)} %k_ref.1) | copy-start | bytes 786436
  2.5 0.9 %copy-start.2 = (bf16[256,512]{1,0:T(8,128)(2,1)S(1)}, bf16[256,512]{1,0:T(8,128)(2,1)}, u32[]{:S(2)}) copy-start(bf16[256,512]{1,0:T(8,128)(2,1)} %v_ref.1) | copy-start | bytes 786436
  3.5 0.9 %copy-start.3 = (bf16[64,2048]{1,0:T(8,128)(2,1)S(1)}, bf16[64,2048]{1,0:T(8,128)(2,1)}, u32[]{:S(2)}) copy-start(bf16[64,2048]{1,0:T(8,128)(2,1)} %og_ref.1) | copy-start | bytes 786436

commit v2 on v1

v2 whole, which is shorter than its diff:
```python
import functools

import jax
import jax.numpy as jnp
from jax import lax
from jax.experimental import pallas as pl
from jax.experimental.pallas import tpu as pltpu
from jax.sharding import PartitionSpec as P

HEAD_DIM = 128
STRIDE = 256
TILE = 16
PAIRS = TILE // 2
HALF = 32
NEG_LARGE = -1e30
SCALE = HEAD_DIM**-0.5
STEP = 1
EARLY = 40
MESH = pl.DeviceIdType.MESH
F32 = jnp.float32
BF16 = jnp.bfloat16


def dot_nt(a, b):
    return lax.dot_general(a, b, (((1,), (1,)), ((), ())), preferred_element_type=F32)


def dot_nn(a, b):
    return lax.dot_general(a, b, (((1,), (0,)), ((), ())), preferred_element_type=F32)


def dot_tn(a, b):
    return lax.dot_general(a, b, (((0,), (0,)), ((), ())), preferred_element_type=F32)


def dot_exact(a, b):
    return lax.dot_general(
        a, b, (((1,), (0,)), ((), ())),
        preferred_element_type=F32, precision=lax.Precision.HIGHEST,
    )


def iota(shape, axis):
    return lax.broadcasted_iota(jnp.int32, shape, axis)


def combine(top, total, weighted, other_top, other_total, other_weighted):
    peak = jnp.maximum(top, other_top)
    mine, theirs = jnp.exp(top - peak), jnp.exp(other_top - peak)
    inverse = 1.0 / (total * mine + other_total * theirs)
    return mine * inverse, (weighted * mine + other_weighted * theirs) * inverse


def kernel(
    seq_count, head_count,
    q_hbm, k_hbm, v_hbm, og_hbm,
    dq_ref, dk_ref, dv_ref,
    q_ref, kv_ref, og_ref, g_home, halo, back_snd, back_rcv,
    snd, rcv, gsnd, grcv, stat_snd, stat_rcv, cstat_snd, cstat_rcv, grad_snd, grad_rcv,
    classes, class_grad, class_e, class_pg, class_row,
    e_diag, e_prev, pg_diag, pg_prev, stat_row, cstat_row, acc,
    load_sem, g_send_sem, g_recv_sem, halo_send_sem, halo_recv_sem, back_send_sem, back_recv_sem,
    send_sem, recv_sem,
):
    s = lax.axis_index("seq")
    hd = lax.axis_index("head")
    others = seq_count - 1
    width = q_ref.shape[1]
    heads = width // HEAD_DIM
    tiles = STRIDE // TILE
    chunks = seq_count // TILE
    after = lax.rem(s + 1, seq_count)
    before = lax.rem(s + seq_count - 1, seq_count)
    part = og_ref.shape[0]

    loads = [
        pltpu.make_async_copy(src, dst, load_sem.at[i])
        for i, (src, dst) in enumerate(
            ((q_hbm, q_ref), (k_hbm, kv_ref.at[0]), (v_hbm, kv_ref.at[1]), (og_hbm, og_ref))
        )
    ]
    for load in loads:
        load.start()

    barrier = pltpu.get_barrier_semaphore()

    @pl.loop(1, seq_count)
    def _(i):
        pl.semaphore_signal(
            barrier, inc=1, device_id=(lax.rem(s + i, seq_count), hd), device_id_type=MESH
        )

    @pl.loop(1, head_count)
    def _(i):
        pl.semaphore_signal(
            barrier, inc=1, device_id=(s, lax.rem(hd + i, head_count)), device_id_type=MESH
        )

    for load in loads:
        load.wait()
    for j, ref in enumerate((q_ref, kv_ref.at[0], kv_ref.at[1])):
        for h in range(heads):
            snd[h * tiles : (h + 1) * tiles, j] = ref[
                :, h * HEAD_DIM : (h + 1) * HEAD_DIM
            ].reshape(tiles, TILE, HEAD_DIM)
    rcv[s] = snd[s]
    own_rows = pl.ds(pl.multiple_of(hd * part, part), part)
    g_home[own_rows, :] = og_ref[:, pl.ds(pl.multiple_of(hd * width, width), width)]

    pl.semaphore_wait(barrier, others + head_count - 1)

    def send(src, dst, index, i):
        peer = lax.rem(s + i * STEP, seq_count)
        pltpu.make_async_remote_copy(
            src_ref=src.at[peer],
            dst_ref=dst.at[s],
            send_sem=send_sem.at[index],
            recv_sem=recv_sem.at[index],
            device_id=(peer, hd),
            device_id_type=MESH,
        ).start()

    def whole(src, dst, index):
        return pltpu.make_async_remote_copy(
            src_ref=src.at[pl.ds(0, others)],
            dst_ref=dst.at[pl.ds(0, others)],
            send_sem=send_sem.at[index],
            recv_sem=recv_sem.at[index],
            device_id=(after, hd),
            device_id_type=MESH,
        )

    def strip(src, dst, send, recv, peer, i):
        rows = pl.ds(pl.multiple_of(i * TILE, TILE), TILE)
        pltpu.make_async_remote_copy(
            src_ref=src.at[:, rows, :],
            dst_ref=dst.at[:, rows, :],
            send_sem=send,
            recv_sem=recv,
            device_id=(peer, hd),
            device_id_type=MESH,
        ).start()

    def strips(src, dst, send, recv, peer):
        return pltpu.make_async_remote_copy(
            src_ref=src, dst_ref=dst, send_sem=send, recv_sem=recv,
            device_id=(peer, hd), device_id_type=MESH,
        )

    g_copies = []
    for i in range(1, head_count):
        peer = lax.rem(hd + i, head_count)
        copy = pltpu.make_async_remote_copy(
            src_ref=og_ref.at[:, pl.ds(pl.multiple_of(peer * width, width), width)],
            dst_ref=g_home.at[own_rows, :],
            send_sem=g_send_sem.at[i],
            recv_sem=g_recv_sem.at[i],
            device_id=(s, peer),
            device_id_type=MESH,
        )
        copy.start()
        g_copies.append(copy)

    @pl.loop(0, tiles)
    def _(i):
        strip(kv_ref, halo, halo_send_sem, halo_recv_sem, after, i)
        for n in range(4):
            if n < 3:
                send(snd, rcv, 0, 1 + i * 3 + n)

    @pl.loop(1 + 3 * tiles, seq_count)
    def _(i):
        send(snd, rcv, 0, i)

    for copy in g_copies:
        copy.wait_recv()
    for h in range(heads):
        gsnd[h * tiles : (h + 1) * tiles] = g_home[
            :, h * HEAD_DIM : (h + 1) * HEAD_DIM
        ].reshape(tiles, TILE, HEAD_DIM)

    @pl.loop(1, seq_count)
    def _(i):
        send(gsnd, grcv, 1, i)

    grcv[s] = gsnd[s]

    strips(kv_ref, halo, halo_send_sem, halo_recv_sem, after).wait_recv()

    row = iota((STRIDE, STRIDE), 0)
    col = iota((STRIDE, STRIDE), 1)

    @pl.loop(0, heads)
    def _(h):
        at = pl.ds(pl.multiple_of(h * HEAD_DIM, HEAD_DIM), HEAD_DIM)
        qh, gh = q_ref[:, at], g_home[:, at]
        sd = jnp.where(row <= col, dot_nt(kv_ref[0, :, at], qh) * SCALE, NEG_LARGE)
        sp = jnp.where((row > col) & (s > 0), dot_nt(halo[0, :, at], qh) * SCALE, NEG_LARGE)
        top = jnp.maximum(
            jnp.max(sd, axis=0, keepdims=True), jnp.max(sp, axis=0, keepdims=True)
        )
        ed, ep = jnp.exp(sd - top), jnp.exp(sp - top)
        gd, gp = dot_nt(kv_ref[1, :, at], gh), dot_nt(halo[1, :, at], gh)
        e_diag[h], e_prev[h], pg_diag[h], pg_prev[h] = ed, ep, gd, gp
        total = jnp.sum(ed + ep, axis=0, keepdims=True)
        weighted = jnp.sum(ed * gd + ep * gp, axis=0, keepdims=True)
        for n, value in enumerate((top, total, weighted)):
            stat_row[n, pl.ds(h, 1), :] = value

    owner = lax.rem(iota((seq_count, STRIDE), 0), tiles) == iota((seq_count, STRIDE), 1) // TILE
    code_row = lax.rem(iota((STRIDE, HEAD_DIM), 0), TILE)
    code_row = lax.rem(code_row, 2) * HALF + code_row // 2
    pick_lane = iota((STRIDE, HEAD_DIM), 1)
    code_col = lax.rem(iota((HEAD_DIM, STRIDE), 1), TILE)
    code_col = lax.rem(code_col, 2) * HALF + code_col // 2
    pick_row = iota((HEAD_DIM, STRIDE), 0)

    coded = jnp.zeros((seq_count, HEAD_DIM), F32)
    for n in range(3):
        values = jnp.broadcast_to(
            stat_row[n][:, None, :], (heads, tiles, STRIDE)
        ).reshape(seq_count, STRIDE)
        select = (pick_lane == code_row + n * PAIRS).astype(F32)
        coded = coded + dot_exact(jnp.where(owner, values, 0.0), select)
    stat_snd[:, 0, :] = coded
    stat_rcv[s] = stat_snd[s]

    @pl.loop(1, seq_count)
    def _(i):
        send(stat_snd, stat_rcv, 2, i)

    swap_row = iota((STRIDE, STRIDE), 0)
    swap_col = iota((STRIDE, STRIDE), 1)
    swap = (
        (swap_row // TILE == lax.rem(swap_col, TILE))
        & (lax.rem(swap_row, TILE) == swap_col // TILE)
    ).astype(BF16)

    whole(snd, rcv, 0).wait_recv()
    whole(gsnd, grcv, 1).wait_recv()
    for c in range(chunks):
        these = slice(c * TILE, (c + 1) * TILE)
        mixed = jnp.concatenate(
            [rcv[these, j].reshape(STRIDE, HEAD_DIM) for j in range(3)]
            + [grcv[these].reshape(STRIDE, HEAD_DIM)],
            axis=1,
        )
        sorted_rows = dot_nn(swap, mixed).astype(BF16)
        for j in range(4):
            classes[j, :, these, :] = sorted_rows[:, j * HEAD_DIM : (j + 1) * HEAD_DIM].reshape(
                TILE, TILE, HEAD_DIM
            )

    pair = 2 * seq_count
    prow = iota((pair, pair), 0)
    pcol = iota((pair, pair), 1)
    allowed = ((prow < seq_count) == (pcol < seq_count)) & (prow < pcol)

    def pair_of(j, p):
        return classes[j, 2 * p : 2 * p + 2].reshape(pair, HEAD_DIM)

    class_row[...] = jnp.zeros_like(class_row)
    for p in range(PAIRS):
        sc = jnp.where(allowed, dot_nt(pair_of(1, p), pair_of(0, p)) * SCALE, NEG_LARGE)
        pg = dot_nt(pair_of(2, p), pair_of(3, p))
        top = jnp.max(sc, axis=0, keepdims=True)
        ec = jnp.where(allowed, jnp.exp(sc - top), 0.0)
        class_e[p], class_pg[p] = ec, pg
        total = jnp.sum(ec, axis=0, keepdims=True)
        weighted = jnp.sum(ec * pg, axis=0, keepdims=True)
        for n, value in enumerate((top, total, weighted)):
            class_row[n * PAIRS + p : n * PAIRS + p + 1, :] = value
    columns = class_row[...].T
    small = iota((seq_count, HEAD_DIM), 1) < HALF
    cstat_snd[:, 0, :] = jnp.where(
        small, columns[:seq_count], pltpu.roll(columns[seq_count:], HALF, 1)
    )
    cstat_rcv[s] = cstat_snd[s]

    @pl.loop(1, seq_count)
    def _(i):
        send(cstat_snd, cstat_rcv, 3, i)

    whole(stat_snd, stat_rcv, 2).wait_recv()
    band = stat_rcv[:, 0, :]
    band_row = jnp.concatenate([band, pltpu.roll(band, HEAD_DIM - HALF, 1)], axis=0).T
    for p in range(PAIRS):
        factor, delta = combine(
            *(class_row[n * PAIRS + p : n * PAIRS + p + 1, :] for n in range(3)),
            *(band_row[n * PAIRS + p : n * PAIRS + p + 1, :] for n in range(3)),
        )
        probs = class_e[p] * factor
        sgrad = (probs * (class_pg[p] - delta)).astype(BF16)
        for j, value in enumerate(
            (
                dot_tn(sgrad, pair_of(1, p)) * SCALE,
                dot_nn(sgrad, pair_of(0, p)) * SCALE,
                dot_nn(probs.astype(BF16), pair_of(3, p)),
            )
        ):
            class_grad[j, 2 * p : 2 * p + 2] = value.astype(BF16).reshape(
                2, seq_count, HEAD_DIM
            )
    for c in range(chunks):
        these = slice(c * TILE, (c + 1) * TILE)
        mixed = jnp.concatenate(
            [class_grad[j, :, these, :].reshape(STRIDE, HEAD_DIM) for j in range(3)], axis=1
        )
        sorted_rows = dot_nn(swap, mixed).astype(BF16)
        for j in range(3):
            grad_snd[these, j] = sorted_rows[:, j * HEAD_DIM : (j + 1) * HEAD_DIM].reshape(
                TILE, TILE, HEAD_DIM
            )
    grad_rcv[s] = grad_snd[s]

    @pl.loop(1, EARLY)
    def _(i):
        send(grad_snd, grad_rcv, 4, i)

    whole(cstat_snd, cstat_rcv, 3).wait_recv()
    got = cstat_rcv[:, 0, :]
    for n in range(3):
        select = (pick_row == code_col + n * PAIRS).astype(F32)
        cstat_row[n] = jnp.sum(
            jnp.where(owner, dot_exact(got, select), 0.0).reshape(heads, tiles, STRIDE), axis=1
        )

    @pl.loop(0, heads)
    def _(h):
        at = pl.ds(pl.multiple_of(h * HEAD_DIM, HEAD_DIM), HEAD_DIM)
        factor, delta = combine(
            *(stat_row[n, pl.ds(h, 1), :] for n in range(3)),
            *(cstat_row[n, pl.ds(h, 1), :] for n in range(3)),
        )
        stat_row[0, pl.ds(h, 1), :] = factor
        stat_row[1, pl.ds(h, 1), :] = delta
        probs = e_prev[h] * factor
        sgrad = (probs * (pg_prev[h] - delta)).astype(BF16)
        back_snd[0, :, at] = (dot_nn(sgrad, q_ref[:, at]) * SCALE).astype(BF16)
        back_snd[1, :, at] = dot_nn(probs.astype(BF16), g_home[:, at]).astype(BF16)
        acc[0, :, at] = dot_tn(sgrad, halo[0, :, at])

    @pl.loop(0, tiles)
    def _(i):
        strip(back_snd, back_rcv, back_send_sem, back_recv_sem, before, i)
        send(grad_snd, grad_rcv, 4, EARLY + i)

    @pl.loop(EARLY + tiles, seq_count)
    def _(i):
        send(grad_snd, grad_rcv, 4, i)

    @pl.loop(0, heads)
    def _(h):
        at = pl.ds(pl.multiple_of(h * HEAD_DIM, HEAD_DIM), HEAD_DIM)
        factor, delta = (stat_row[n, pl.ds(h, 1), :] for n in range(2))
        probs = e_diag[h] * factor
        sgrad = (probs * (pg_diag[h] - delta)).astype(BF16)
        acc[0, :, at] = (acc[0, :, at] + dot_tn(sgrad, kv_ref[0, :, at])) * SCALE
        acc[1, :, at] = dot_nn(sgrad, q_ref[:, at]) * SCALE
        acc[2, :, at] = dot_nn(probs.astype(BF16), g_home[:, at])

    whole(grad_snd, grad_rcv, 4).wait_recv()
    back = strips(back_snd, back_rcv, back_send_sem, back_recv_sem, before)
    back.wait_recv()
    for h in range(heads):
        at = slice(h * HEAD_DIM, (h + 1) * HEAD_DIM)
        for j, out in enumerate((dq_ref, dk_ref, dv_ref)):
            value = acc[j, :, at] + grad_rcv[h * tiles : (h + 1) * tiles, j].reshape(
                STRIDE, HEAD_DIM
            ).astype(F32)
            if j > 0:
                value = value + back_rcv[j - 1, :, at].astype(F32)
            out[:, at] = value.astype(BF16)

    for copy in g_copies:
        copy.wait_send()
    strips(kv_ref, halo, halo_send_sem, halo_recv_sem, after).wait_send()
    for index, buffers in enumerate(
        ((snd, rcv), (gsnd, grcv), (stat_snd, stat_rcv), (cstat_snd, cstat_rcv), (grad_snd, grad_rcv))
    ):
        whole(*buffers, index).wait_send()
    back.wait_send()


def per_device(queries, keys, values, out_grad):
    length, width = queries.shape
    seq_count = lax.axis_size("seq")
    head_count = lax.axis_size("head")
    heads = width // HEAD_DIM
    assert length == STRIDE and seq_count * TILE == STRIDE * heads and seq_count * 2 == HEAD_DIM
    vmem = pl.BlockSpec(memory_space=pltpu.VMEM)
    far = pl.BlockSpec(memory_space=pltpu.HBM)
    tile = (TILE, HEAD_DIM)
    pair = 2 * seq_count
    return pl.pallas_call(
        functools.partial(kernel, seq_count, head_count),
        out_shape=[jax.ShapeDtypeStruct(queries.shape, BF16)] * 3,
        in_specs=[far] * 4,
        out_specs=[vmem] * 3,
        scratch_shapes=[
            pltpu.VMEM((length, width), BF16),
            pltpu.VMEM((2, length, width), BF16),
            pltpu.VMEM(out_grad.shape, BF16),
            pltpu.VMEM((length, width), BF16),
            pltpu.VMEM((2, length, width), BF16),
            pltpu.VMEM((2, length, width), BF16),
            pltpu.VMEM((2, length, width), BF16),
            pltpu.VMEM((seq_count, 3) + tile, BF16),
            pltpu.VMEM((seq_count, 3) + tile, BF16),
            pltpu.VMEM((seq_count,) + tile, BF16),
            pltpu.VMEM((seq_count,) + tile, BF16),
            pltpu.VMEM((seq_count, 1, HEAD_DIM), F32),
            pltpu.VMEM((seq_count, 1, HEAD_DIM), F32),
            pltpu.VMEM((seq_count, 1, HEAD_DIM), F32),
            pltpu.VMEM((seq_count, 1, HEAD_DIM), F32),
            pltpu.VMEM((seq_count, 3) + tile, BF16),
            pltpu.VMEM((seq_count, 3) + tile, BF16),
            pltpu.VMEM((4, TILE, seq_count, HEAD_DIM), BF16),
            pltpu.VMEM((3, TILE, seq_count, HEAD_DIM), BF16),
            pltpu.VMEM((PAIRS, pair, pair), F32),
            pltpu.VMEM((PAIRS, pair, pair), F32),
            pltpu.VMEM((HEAD_DIM, HEAD_DIM), F32),
            pltpu.VMEM((heads, STRIDE, STRIDE), F32),
            pltpu.VMEM((heads, STRIDE, STRIDE), F32),
            pltpu.VMEM((heads, STRIDE, STRIDE), F32),
            pltpu.VMEM((heads, STRIDE, STRIDE), F32),
            pltpu.VMEM((3, heads, STRIDE), F32),
            pltpu.VMEM((3, heads, STRIDE), F32),
            pltpu.VMEM((3, length, width), F32),
            pltpu.SemaphoreType.DMA((4,)),
            pltpu.SemaphoreType.DMA((head_count,)),
            pltpu.SemaphoreType.DMA((head_count,)),
            pltpu.SemaphoreType.DMA,
            pltpu.SemaphoreType.DMA,
            pltpu.SemaphoreType.DMA,
            pltpu.SemaphoreType.DMA,
            pltpu.SemaphoreType.DMA((5,)),
            pltpu.SemaphoreType.DMA((5,)),
        ],
        compiler_params=pltpu.CompilerParams(
            collective_id=0, has_side_effects=True, vmem_limit_bytes=62 * 2**20
        ),
    )(queries, keys, values, out_grad)


def solution(mesh):
    return jax.shard_map(
        per_device,
        mesh=mesh,
        in_specs=(P("seq", "head"), P("seq", "head"), P("seq", "head"), P(("seq", "head"), None)),
        out_specs=(P("seq", "head"), P("seq", "head"), P("seq", "head")),
        check_vma=False,
    )
```

time: 95.8 us -> 84.3 us (0.88); the launches traced: 94.3 us -> 83.8 us
  Pallas kernels: 87.7 us -> 79.7 us
  local copies, waits for them, and re-layouts: 5.9 us -> 3.46 us
    pallas_call x1, Pallas kernels: 87.7 us -> 79.7 us  [per_device(): pl.pallas_call(functools.partial(kernel, seq_count, head_count), out_shap...]
    unnamed x11 -> x7, local copies, waits for them, and re-layouts: 5.9 us -> 3.46 us
where the time goes in v2:
time: 84.3 us; the launch traced here: 83.8 us
  Pallas kernels  79.7 us (95%)
  local copies, waits for them, and re-layouts  3.46 us (4%)
    pallas_call x1, Pallas kernels, per_device(): pl.pallas_call(functools.partial(kernel, seq_count, head_count), out_shap...  79.7 us
    unnamed x7, local copies, waits for them, and re-layouts  3.46 us

profile of v2, /device:TPU:24, one launch (start us, length us, event | category | flops | bytes accessed | tf_op | source)
XLA Modules:
  0.0 83.8 jit_solution(10070347862310968357)
XLA Ops:
  0.6 79.7 %shard_map.67 = (bf16[256,512]{1,0:T(8,128)(2,1)}, bf16[256,512]{1,0:T(8,128)(2,1)}, bf16[256,512]{1,0:T(8,128)(2,1)}) custom-call(bf16[256,512]{1,0:T(8,128)(2,1)} %q_hbm.1, bf16[256,512]{1,0:T(8,128)(2,1)} %k_hbm.1, bf16[256,512]{1,0:T(8,128)(2,1)} %v_hbm.1, bf16[64,2048]{1,0:T(8,128)(2,1)} %og_hbm.1), custom_call_target="tpu_custom_call" | custom-call | tf_op jit(solution)/shard_map/pallas_call | solution.py:395
  80.4 0.0 copy-start.1
  80.4 1.7 %copy.10 = bf16[256,512]{1,0:T(8,128)(2,1)} copy(bf16[256,512]{1,0:T(8,128)(2,1)} %get-tuple-element.6) | data formatting | bytes 524288
  82.1 0.0 copy-done.1
  82.1 0.0 copy-start
  82.1 0.7 copy.11
  82.8 0.3 copy-done
  83.1 0.7 copy.12
Async XLA Ops:
  80.4 1.7 %copy-start.1 = (bf16[256,512]{1,0:T(8,128)(2,1)S(1)}, bf16[256,512]{1,0:T(8,128)(2,1)}, u32[]{:S(2)}) copy-start(bf16[256,512]{1,0:T(8,128)(2,1)} %get-tuple-element.7) | copy-start | bytes 786436
  82.1 1.0 %copy-start = (bf16[256,512]{1,0:T(8,128)(2,1)S(1)}, bf16[256,512]{1,0:T(8,128)(2,1)}, u32[]{:S(2)}) copy-start(bf16[256,512]{1,0:T(8,128)(2,1)} %get-tuple-element.8) | copy-start | bytes 786436

commit v3 on v2

--- a/solution.py
+++ b/solution.py
@@ -14,8 +14,8 @@
 HALF = 32
 NEG_LARGE = -1e30
 SCALE = HEAD_DIM**-0.5
-STEP = 1
 EARLY = 40
+LAG = 3
 MESH = pl.DeviceIdType.MESH
 F32 = jnp.float32
 BF16 = jnp.bfloat16
@@ -55,30 +55,34 @@
     seq_count, head_count,
     q_hbm, k_hbm, v_hbm, og_hbm,
     dq_ref, dk_ref, dv_ref,
-    q_ref, kv_ref, og_ref, g_home, halo, back_snd, back_rcv,
+    q_ref, kv_ref, og_ref, g_home, halo, relay, back_snd, back_rcv, back_relay,
     snd, rcv, gsnd, grcv, stat_snd, stat_rcv, cstat_snd, cstat_rcv, grad_snd, grad_rcv,
     classes, class_grad, class_e, class_pg, class_row,
     e_diag, e_prev, pg_diag, pg_prev, stat_row, cstat_row, acc,
-    load_sem, g_send_sem, g_recv_sem, halo_send_sem, halo_recv_sem, back_send_sem, back_recv_sem,
-    send_sem, recv_sem,
+    load_sem, g_send_sem, g_recv_sem, halo_send_sem, halo_recv_sem, relay_sem, back_send_sem, back_recv_sem, back_relay_sem,
+    pass_send_sem, send_sem, recv_sem,
 ):
     s = lax.axis_index("seq")
     hd = lax.axis_index("head")
     others = seq_count - 1
-    width = q_ref.shape[1]
-    heads = width // HEAD_DIM
+    heads = q_ref.shape[0]
+    width = heads * HEAD_DIM
     tiles = STRIDE // TILE
     chunks = seq_count // TILE
     after = lax.rem(s + 1, seq_count)
-    before = lax.rem(s + seq_count - 1, seq_count)
     part = og_ref.shape[0]
 
-    loads = [
-        pltpu.make_async_copy(src, dst, load_sem.at[i])
-        for i, (src, dst) in enumerate(
-            ((q_hbm, q_ref), (k_hbm, kv_ref.at[0]), (v_hbm, kv_ref.at[1]), (og_hbm, og_ref))
-        )
-    ]
+    def head_lanes(h):
+        return slice(h * HEAD_DIM, (h + 1) * HEAD_DIM)
+
+    loads = [pltpu.make_async_copy(og_hbm, og_ref, load_sem.at[0])]
+    for h in range(heads):
+        for j, (src, dst) in enumerate(
+            ((q_hbm, q_ref.at[h]), (k_hbm, kv_ref.at[h, 0]), (v_hbm, kv_ref.at[h, 1]))
+        ):
+            loads.append(
+                pltpu.make_async_copy(src.at[:, head_lanes(h)], dst, load_sem.at[1 + 3 * h + j])
+            )
     for load in loads:
         load.start()
 
@@ -98,11 +102,9 @@
 
     for load in loads:
         load.wait()
-    for j, ref in enumerate((q_ref, kv_ref.at[0], kv_ref.at[1])):
-        for h in range(heads):
-            snd[h * tiles : (h + 1) * tiles, j] = ref[
-                :, h * HEAD_DIM : (h + 1) * HEAD_DIM
-            ].reshape(tiles, TILE, HEAD_DIM)
+    for h in range(heads):
+        for j, ref in enumerate((q_ref.at[h], kv_ref.at[h, 0], kv_ref.at[h, 1])):
+            snd[h * tiles : (h + 1) * tiles, j] = ref[...].reshape(tiles, TILE, HEAD_DIM)
     rcv[s] = snd[s]
     own_rows = pl.ds(pl.multiple_of(hd * part, part), part)
     g_home[own_rows, :] = og_ref[:, pl.ds(pl.multiple_of(hd * width, width), width)]
@@ -110,7 +112,7 @@
     pl.semaphore_wait(barrier, others + head_count - 1)
 
     def send(src, dst, index, i):
-        peer = lax.rem(s + i * STEP, seq_count)
+        peer = lax.rem(s + i, seq_count)
         pltpu.make_async_remote_copy(
             src_ref=src.at[peer],
             dst_ref=dst.at[s],
@@ -130,22 +132,89 @@
             device_id_type=MESH,
         )
 
-    def strip(src, dst, send, recv, peer, i):
-        rows = pl.ds(pl.multiple_of(i * TILE, TILE), TILE)
-        pltpu.make_async_remote_copy(
-            src_ref=src.at[:, rows, :],
-            dst_ref=dst.at[:, rows, :],
+    odd = lax.rem(s, 2) == 1
+    even = lax.rem(s, 2) == 0
+    direct = heads // 2
+
+    def hop(src, dst, at, send, recv, distance):
+        return pltpu.make_async_remote_copy(
+            src_ref=src.at[at],
+            dst_ref=dst.at[at],
             send_sem=send,
             recv_sem=recv,
-            device_id=(peer, hd),
+            device_id=(lax.rem(s + distance + seq_count, seq_count), hd),
             device_id_type=MESH,
-        ).start()
-
-    def strips(src, dst, send, recv, peer):
+        )
+
+    def hop_relay(src, dst, at, send, recv, distance, to_relay):
+        there = (at[0] - direct, at[1])
+        return pltpu.make_async_remote_copy(
+            src_ref=src.at[at] if to_relay else src.at[there],
+            dst_ref=dst.at[there] if to_relay else dst.at[at],
+            send_sem=send,
+            recv_sem=recv,
+            device_id=(lax.rem(s + distance + seq_count, seq_count), hd),
+            device_id_type=MESH,
+        )
+
+    def halo_hop(at):
+        straight = hop(kv_ref, halo, at, halo_send_sem, halo_recv_sem, 1)
+        if at[0] < direct:
+            straight.start()
+            return
+
+        @pl.when(even)
+        def _():
+            straight.start()
+
+        @pl.when(odd)
+        def _():
+            halo_to_relay(at).start()
+
+    def halo_to_relay(at):
+        sem = relay_sem.at[at[0] - direct, at[1]]
+        return hop_relay(kv_ref, relay, at, halo_send_sem, sem, -1, True)
+
+    def halo_pass(at):
+        @pl.when(even)
+        def _():
+            halo_to_relay(at).wait_recv()
+            hop_relay(relay, halo, at, pass_send_sem.at[0], halo_recv_sem, 2, False).start()
+
+    def back_hop(at):
+        straight = hop(back_snd, back_rcv, at, back_send_sem, back_recv_sem, -1)
+        if at[0] < direct:
+            straight.start()
+            return
+
+        @pl.when(odd)
+        def _():
+            straight.start()
+
+        @pl.when(even)
+        def _():
+            back_to_relay(at).start()
+
+    def back_to_relay(at):
+        sem = back_relay_sem.at[at[0] - direct, at[1]]
+        return hop_relay(back_snd, back_relay, at, back_send_sem, sem, 1, True)
+
+    def back_pass(at):
+        @pl.when(odd)
+        def _():
+            back_to_relay(at).wait_recv()
+            hop_relay(back_relay, back_rcv, at, pass_send_sem.at[1], back_recv_sem, -2, False).start()
+
+    def hop_all(src, dst, send, recv):
         return pltpu.make_async_remote_copy(
             src_ref=src, dst_ref=dst, send_sem=send, recv_sem=recv,
-            device_id=(peer, hd), device_id_type=MESH,
-        )
+            device_id=(after, hd), device_id_type=MESH,
+        )
+
+    passed = [(h, j) for h in range(direct, heads) for j in range(2)]
+    kept = [(h, j) for h in range(direct) for j in range(2)]
+    halo_all = hop_all(kv_ref, halo, halo_send_sem, halo_recv_sem)
+    back_all = hop_all(back_snd, back_rcv, back_send_sem, back_recv_sem)
 
     g_copies = []
     for i in range(1, head_count):
@@ -161,17 +230,17 @@
         copy.start()
         g_copies.append(copy)
 
-    @pl.loop(0, tiles)
-    def _(i):
-        strip(kv_ref, halo, halo_send_sem, halo_recv_sem, after, i)
-        for n in range(4):
-            if n < 3:
-                send(snd, rcv, 0, 1 + i * 3 + n)
-
-    @pl.loop(1 + 3 * tiles, seq_count)
-    def _(i):
-        send(snd, rcv, 0, i)
-
+    blocks = passed + kept
+    share = seq_count // len(blocks)
+    for n, at in enumerate(blocks):
+        halo_hop(at)
+
+        @pl.loop(max(1, n * share), (n + 1) * share)
+        def _(i):
+            send(snd, rcv, 0, i)
+
+        if n >= LAG and n - LAG < len(passed):
+            halo_pass(blocks[n - LAG])
     for copy in g_copies:
         copy.wait_recv()
     for h in range(heads):
@@ -185,22 +254,24 @@
 
     grcv[s] = gsnd[s]
 
-    strips(kv_ref, halo, halo_send_sem, halo_recv_sem, after).wait_recv()
+    halo_all.wait_recv()
 
     row = iota((STRIDE, STRIDE), 0)
     col = iota((STRIDE, STRIDE), 1)
 
+    def lanes_of(h):
+        return pl.ds(pl.multiple_of(h * HEAD_DIM, HEAD_DIM), HEAD_DIM)
+
     @pl.loop(0, heads)
     def _(h):
-        at = pl.ds(pl.multiple_of(h * HEAD_DIM, HEAD_DIM), HEAD_DIM)
-        qh, gh = q_ref[:, at], g_home[:, at]
-        sd = jnp.where(row <= col, dot_nt(kv_ref[0, :, at], qh) * SCALE, NEG_LARGE)
-        sp = jnp.where((row > col) & (s > 0), dot_nt(halo[0, :, at], qh) * SCALE, NEG_LARGE)
+        qh, gh = q_ref[h], g_home[:, lanes_of(h)]
+        sd = jnp.where(row <= col, dot_nt(kv_ref[h, 0], qh) * SCALE, NEG_LARGE)
+        sp = jnp.where((row > col) & (s > 0), dot_nt(halo[h, 0], qh) * SCALE, NEG_LARGE)
         top = jnp.maximum(
             jnp.max(sd, axis=0, keepdims=True), jnp.max(sp, axis=0, keepdims=True)
         )
         ed, ep = jnp.exp(sd - top), jnp.exp(sp - top)
-        gd, gp = dot_nt(kv_ref[1, :, at], gh), dot_nt(halo[1, :, at], gh)
+        gd, gp = dot_nt(kv_ref[h, 1], gh), dot_nt(halo[h, 1], gh)
         e_diag[h], e_prev[h], pg_diag[h], pg_prev[h] = ed, ep, gd, gp
         total = jnp.sum(ed + ep, axis=0, keepdims=True)
         weighted = jnp.sum(ed * gd + ep * gp, axis=0, keepdims=True)
@@ -237,19 +308,20 @@
     ).astype(BF16)
 
     whole(snd, rcv, 0).wait_recv()
-    whole(gsnd, grcv, 1).wait_recv()
-    for c in range(chunks):
-        these = slice(c * TILE, (c + 1) * TILE)
-        mixed = jnp.concatenate(
-            [rcv[these, j].reshape(STRIDE, HEAD_DIM) for j in range(3)]
-            + [grcv[these].reshape(STRIDE, HEAD_DIM)],
-            axis=1,
-        )
-        sorted_rows = dot_nn(swap, mixed).astype(BF16)
-        for j in range(4):
-            classes[j, :, these, :] = sorted_rows[:, j * HEAD_DIM : (j + 1) * HEAD_DIM].reshape(
-                TILE, TILE, HEAD_DIM
+
+    def sort_classes(blocks, first):
+        for c in range(chunks):
+            these = slice(c * TILE, (c + 1) * TILE)
+            mixed = jnp.concatenate(
+                [block(these).reshape(STRIDE, HEAD_DIM) for block in blocks], axis=1
             )
+            sorted_rows = dot_nn(swap, mixed).astype(BF16)
+            for j in range(len(blocks)):
+                classes[first + j, :, these, :] = sorted_rows[
+                    :, j * HEAD_DIM : (j + 1) * HEAD_DIM
+                ].reshape(TILE, TILE, HEAD_DIM)
+
+    sort_classes([lambda these, j=j: rcv[these, j] for j in range(3)], 0)
 
     pair = 2 * seq_count
     prow = iota((pair, pair), 0)
@@ -262,14 +334,20 @@
     class_row[...] = jnp.zeros_like(class_row)
     for p in range(PAIRS):
         sc = jnp.where(allowed, dot_nt(pair_of(1, p), pair_of(0, p)) * SCALE, NEG_LARGE)
-        pg = dot_nt(pair_of(2, p), pair_of(3, p))
         top = jnp.max(sc, axis=0, keepdims=True)
         ec = jnp.where(allowed, jnp.exp(sc - top), 0.0)
-        class_e[p], class_pg[p] = ec, pg
-        total = jnp.sum(ec, axis=0, keepdims=True)
-        weighted = jnp.sum(ec * pg, axis=0, keepdims=True)
-        for n, value in enumerate((top, total, weighted)):
-            class_row[n * PAIRS + p : n * PAIRS + p + 1, :] = value
+        class_e[p] = ec
+        class_row[p : p + 1, :] = top
+        class_row[PAIRS + p : PAIRS + p + 1, :] = jnp.sum(ec, axis=0, keepdims=True)
+
+    whole(gsnd, grcv, 1).wait_recv()
+    sort_classes([lambda these: grcv[these]], 3)
+    for p in range(PAIRS):
+        pg = dot_nt(pair_of(2, p), pair_of(3, p))
+        class_pg[p] = pg
+        class_row[2 * PAIRS + p : 2 * PAIRS + p + 1, :] = jnp.sum(
+            class_e[p] * pg, axis=0, keepdims=True
+        )
     columns = class_row[...].T
     small = iota((seq_count, HEAD_DIM), 1) < HALF
     cstat_snd[:, 0, :] = jnp.where(
@@ -325,61 +403,73 @@
             jnp.where(owner, dot_exact(got, select), 0.0).reshape(heads, tiles, STRIDE), axis=1
         )
 
-    @pl.loop(0, heads)
-    def _(h):
-        at = pl.ds(pl.multiple_of(h * HEAD_DIM, HEAD_DIM), HEAD_DIM)
+    def band_prev(h):
         factor, delta = combine(
-            *(stat_row[n, pl.ds(h, 1), :] for n in range(3)),
-            *(cstat_row[n, pl.ds(h, 1), :] for n in range(3)),
-        )
-        stat_row[0, pl.ds(h, 1), :] = factor
-        stat_row[1, pl.ds(h, 1), :] = delta
+            *(stat_row[n, h : h + 1, :] for n in range(3)),
+            *(cstat_row[n, h : h + 1, :] for n in range(3)),
+        )
+        stat_row[0, h : h + 1, :] = factor
+        stat_row[1, h : h + 1, :] = delta
         probs = e_prev[h] * factor
         sgrad = (probs * (pg_prev[h] - delta)).astype(BF16)
-        back_snd[0, :, at] = (dot_nn(sgrad, q_ref[:, at]) * SCALE).astype(BF16)
-        back_snd[1, :, at] = dot_nn(probs.astype(BF16), g_home[:, at]).astype(BF16)
-        acc[0, :, at] = dot_tn(sgrad, halo[0, :, at])
-
-    @pl.loop(0, tiles)
-    def _(i):
-        strip(back_snd, back_rcv, back_send_sem, back_recv_sem, before, i)
-        send(grad_snd, grad_rcv, 4, EARLY + i)
-
-    @pl.loop(EARLY + tiles, seq_count)
-    def _(i):
-        send(grad_snd, grad_rcv, 4, i)
-
-    @pl.loop(0, heads)
-    def _(h):
-        at = pl.ds(pl.multiple_of(h * HEAD_DIM, HEAD_DIM), HEAD_DIM)
-        factor, delta = (stat_row[n, pl.ds(h, 1), :] for n in range(2))
+        back_snd[h, 0] = (dot_nn(sgrad, q_ref[h]) * SCALE).astype(BF16)
+        back_snd[h, 1] = dot_nn(probs.astype(BF16), g_home[:, head_lanes(h)]).astype(BF16)
+        for j in range(2):
+            back_hop((h, j))
+        acc[0, h] = dot_tn(sgrad, halo[h, 0])
+
+    def band_own(h):
+        factor, delta = (stat_row[n, h : h + 1, :] for n in range(2))
         probs = e_diag[h] * factor
         sgrad = (probs * (pg_diag[h] - delta)).astype(BF16)
-        acc[0, :, at] = (acc[0, :, at] + dot_tn(sgrad, kv_ref[0, :, at])) * SCALE
-        acc[1, :, at] = dot_nn(sgrad, q_ref[:, at]) * SCALE
-        acc[2, :, at] = dot_nn(probs.astype(BF16), g_home[:, at])
+        acc[0, h] = (acc[0, h] + dot_tn(sgrad, kv_ref[h, 0])) * SCALE
+        acc[1, h] = dot_nn(sgrad, q_ref[h]) * SCALE
+        acc[2, h] = dot_nn(probs.astype(BF16), g_home[:, head_lanes(h)])
+
+    for h in range(direct, heads):
+        band_prev(h)
+
+    @pl.loop(EARLY, seq_count)
+    def _(i):
+        send(grad_snd, grad_rcv, 4, i)
+
+    for h in range(direct):
+        band_prev(h)
+    for h in range(heads):
+        band_own(h)
+        for at in passed[h * len(passed) // heads : (h + 1) * len(passed) // heads]:
+            back_pass(at)
 
     whole(grad_snd, grad_rcv, 4).wait_recv()
-    back = strips(back_snd, back_rcv, back_send_sem, back_recv_sem, before)
-    back.wait_recv()
+    back_all.wait_recv()
     for h in range(heads):
-        at = slice(h * HEAD_DIM, (h + 1) * HEAD_DIM)
         for j, out in enumerate((dq_ref, dk_ref, dv_ref)):
-            value = acc[j, :, at] + grad_rcv[h * tiles : (h + 1) * tiles, j].reshape(
+            value = acc[j, h] + grad_rcv[h * tiles : (h + 1) * tiles, j].reshape(
                 STRIDE, HEAD_DIM
             ).astype(F32)
             if j > 0:
-                value = value + back_rcv[j - 1, :, at].astype(F32)
-            out[:, at] = value.astype(BF16)
+                value = value + back_rcv[h, j - 1].astype(F32)
+            out[:, head_lanes(h)] = value.astype(BF16)
 
     for copy in g_copies:
         copy.wait_send()
-    strips(kv_ref, halo, halo_send_sem, halo_recv_sem, after).wait_send()
+    halo_all.wait_send()
     for index, buffers in enumerate(
         ((snd, rcv), (gsnd, grcv), (stat_snd, stat_rcv), (cstat_snd, cstat_rcv), (grad_snd, grad_rcv))
     ):
         whole(*buffers, index).wait_send()
-    back.wait_send()
+    back_all.wait_send()
+
+    def sent(src, dst, send, recv):
+        return hop_all(src, dst.at[pl.ds(0, direct)], send, recv)
+
+    @pl.when(even)
+    def _():
+        sent(relay, halo, pass_send_sem.at[0], halo_recv_sem).wait_send()
+
+    @pl.when(odd)
+    def _():
+        sent(back_relay, back_rcv, pass_send_sem.at[1], back_recv_sem).wait_send()
 
 
 def per_device(queries, keys, values, out_grad):
@@ -392,19 +482,21 @@
     far = pl.BlockSpec(memory_space=pltpu.HBM)
     tile = (TILE, HEAD_DIM)
     pair = 2 * seq_count
-    return pl.pallas_call(
+    grads = pl.pallas_call(
         functools.partial(kernel, seq_count, head_count),
-        out_shape=[jax.ShapeDtypeStruct(queries.shape, BF16)] * 3,
+        out_shape=[pltpu.VMEM(queries.shape, BF16)] * 3,
         in_specs=[far] * 4,
         out_specs=[vmem] * 3,
         scratch_shapes=[
-            pltpu.VMEM((length, width), BF16),
-            pltpu.VMEM((2, length, width), BF16),
+            pltpu.VMEM((heads, length, HEAD_DIM), BF16),
+            pltpu.VMEM((heads, 2, length, HEAD_DIM), BF16),
             pltpu.VMEM(out_grad.shape, BF16),
             pltpu.VMEM((length, width), BF16),
-            pltpu.VMEM((2, length, width), BF16),
-            pltpu.VMEM((2, length, width), BF16),
-            pltpu.VMEM((2, length, width), BF16),
+            pltpu.VMEM((heads, 2, length, HEAD_DIM), BF16),
+            pltpu.VMEM((heads // 2, 2, length, HEAD_DIM), BF16),
+            pltpu.VMEM((heads, 2, length, HEAD_DIM), BF16),
+            pltpu.VMEM((heads, 2, length, HEAD_DIM), BF16),
+            pltpu.VMEM((heads // 2, 2, length, HEAD_DIM), BF16),
             pltpu.VMEM((seq_count, 3) + tile, BF16),
             pltpu.VMEM((seq_count, 3) + tile, BF16),
             pltpu.VMEM((seq_count,) + tile, BF16),
@@ -426,14 +518,17 @@
             pltpu.VMEM((heads, STRIDE, STRIDE), F32),
             pltpu.VMEM((3, heads, STRIDE), F32),
             pltpu.VMEM((3, heads, STRIDE), F32),
-            pltpu.VMEM((3, length, width), F32),
-            pltpu.SemaphoreType.DMA((4,)),
+            pltpu.VMEM((3, heads, length, HEAD_DIM), F32),
+            pltpu.SemaphoreType.DMA((1 + 3 * heads,)),
             pltpu.SemaphoreType.DMA((head_count,)),
             pltpu.SemaphoreType.DMA((head_count,)),
             pltpu.SemaphoreType.DMA,
             pltpu.SemaphoreType.DMA,
+            pltpu.SemaphoreType.DMA((heads // 2, 2)),
             pltpu.SemaphoreType.DMA,
             pltpu.SemaphoreType.DMA,
+            pltpu.SemaphoreType.DMA((heads // 2, 2)),
+            pltpu.SemaphoreType.DMA((2,)),
             pltpu.SemaphoreType.DMA((5,)),
             pltpu.SemaphoreType.DMA((5,)),
         ],
@@ -441,6 +536,7 @@
             collective_id=0, has_side_effects=True, vmem_limit_bytes=62 * 2**20
         ),
     )(queries, keys, values, out_grad)
+    return grads
 
 
 def solution(mesh):

time: 84.3 us -> 78.5 us (0.931)
  Pallas kernels: 79.7 us -> 75.6 us
  local copies, waits for them, and re-layouts: 3.46 us -> 2.11 us
    pallas_call x1, Pallas kernels: 79.7 us -> 75.6 us  [per_device(): pl.pallas_call(functools.partial(kernel, seq_count, head_count), out_shap...]
    unnamed x7 -> x3, local copies, waits for them, and re-layouts: 3.46 us -> 2.11 us
where the time goes in v3:
time: 78.5 us; the launch traced here: 78.4 us
  Pallas kernels  75.6 us (96%)
  local copies, waits for them, and re-layouts  2.11 us (3%)
    pallas_call x1, Pallas kernels, per_device(): pl.pallas_call(functools.partial(kernel, seq_count, head_count), out_shap...  75.6 us
    unnamed x3, local copies, waits for them, and re-layouts  2.11 us

profile of v3, /device:TPU:24, one launch (start us, length us, event | category | flops | bytes accessed | tf_op | source)
XLA Modules:
  0.0 78.4 jit_solution(14629417651540869199)
XLA Ops:
  0.6 75.6 %shard_map.67 = (bf16[256,512]{1,0:T(8,128)(2,1)S(1)}, bf16[256,512]{1,0:T(8,128)(2,1)S(1)}, bf16[256,512]{1,0:T(8,128)(2,1)S(1)}) custom-call(bf16[256,512]{1,0:T(8,128)(2,1)} %q_hbm.1, bf16[256,512]{1,0:T(8,128)(2,1)} %k_hbm.1, bf16[256,512]{1,0:T(8,128)(2,1)} %v_hbm.1, bf16[64,2048]{1,0:T(8,128)(2,1)} %og_hbm.1), custom_call_target="tpu_custom_call" | custom-call | tf_op jit(solution)/shard_map/pallas_call | solution.py:485
  76.3 0.7 copy.10
  77.0 0.7 copy.11
  77.7 0.7 copy.12

commit v4 on v3

--- a/solution.py
+++ b/solution.py
@@ -14,8 +14,8 @@
 HALF = 32
 NEG_LARGE = -1e30
 SCALE = HEAD_DIM**-0.5
-EARLY = 40
-LAG = 3
+EARLY = 37
+UNROLL = 9
 MESH = pl.DeviceIdType.MESH
 F32 = jnp.float32
 BF16 = jnp.bfloat16
@@ -54,11 +54,11 @@
 def kernel(
     seq_count, head_count,
     q_hbm, k_hbm, v_hbm, og_hbm,
-    dq_ref, dk_ref, dv_ref,
+    out_ref,
     q_ref, kv_ref, og_ref, g_home, halo, relay, back_snd, back_rcv, back_relay,
     snd, rcv, gsnd, grcv, stat_snd, stat_rcv, cstat_snd, cstat_rcv, grad_snd, grad_rcv,
     classes, class_grad, class_e, class_pg, class_row,
-    e_diag, e_prev, pg_diag, pg_prev, stat_row, cstat_row, acc,
+    e_diag, e_prev, pg_diag, pg_prev, part_row, stat_row, cstat_row, acc,
     load_sem, g_send_sem, g_recv_sem, halo_send_sem, halo_recv_sem, relay_sem, back_send_sem, back_recv_sem, back_relay_sem,
     pass_send_sem, send_sem, recv_sem,
 ):
@@ -88,7 +88,7 @@
 
     barrier = pltpu.get_barrier_semaphore()
 
-    @pl.loop(1, seq_count)
+    @pl.loop(1, seq_count, unroll=UNROLL)
     def _(i):
         pl.semaphore_signal(
             barrier, inc=1, device_id=(lax.rem(s + i, seq_count), hd), device_id_type=MESH
@@ -235,12 +235,10 @@
     for n, at in enumerate(blocks):
         halo_hop(at)
 
-        @pl.loop(max(1, n * share), (n + 1) * share)
+        @pl.loop(max(1, n * share), (n + 1) * share, unroll=True)
         def _(i):
             send(snd, rcv, 0, i)
 
-        if n >= LAG and n - LAG < len(passed):
-            halo_pass(blocks[n - LAG])
     for copy in g_copies:
         copy.wait_recv()
     for h in range(heads):
@@ -248,57 +246,30 @@
             :, h * HEAD_DIM : (h + 1) * HEAD_DIM
         ].reshape(tiles, TILE, HEAD_DIM)
 
-    @pl.loop(1, seq_count)
+    @pl.loop(1, seq_count, unroll=UNROLL)
     def _(i):
         send(gsnd, grcv, 1, i)
 
     grcv[s] = gsnd[s]
-
-    halo_all.wait_recv()
 
     row = iota((STRIDE, STRIDE), 0)
     col = iota((STRIDE, STRIDE), 1)
 
-    def lanes_of(h):
-        return pl.ds(pl.multiple_of(h * HEAD_DIM, HEAD_DIM), HEAD_DIM)
-
-    @pl.loop(0, heads)
-    def _(h):
-        qh, gh = q_ref[h], g_home[:, lanes_of(h)]
-        sd = jnp.where(row <= col, dot_nt(kv_ref[h, 0], qh) * SCALE, NEG_LARGE)
-        sp = jnp.where((row > col) & (s > 0), dot_nt(halo[h, 0], qh) * SCALE, NEG_LARGE)
-        top = jnp.maximum(
-            jnp.max(sd, axis=0, keepdims=True), jnp.max(sp, axis=0, keepdims=True)
-        )
-        ed, ep = jnp.exp(sd - top), jnp.exp(sp - top)
-        gd, gp = dot_nt(kv_ref[h, 1], gh), dot_nt(halo[h, 1], gh)
-        e_diag[h], e_prev[h], pg_diag[h], pg_prev[h] = ed, ep, gd, gp
-        total = jnp.sum(ed + ep, axis=0, keepdims=True)
-        weighted = jnp.sum(ed * gd + ep * gp, axis=0, keepdims=True)
+    def band_part(h, keys, values, mask, e_part, pg_part, part):
+        sc = jnp.where(mask, dot_nt(keys, q_ref[h]) * SCALE, NEG_LARGE)
+        top = jnp.max(sc, axis=0, keepdims=True)
+        ex = jnp.exp(sc - top)
+        pg = dot_nt(values, g_home[:, head_lanes(h)])
+        e_part[h], pg_part[h] = ex, pg
+        total = jnp.sum(ex, axis=0, keepdims=True)
+        weighted = jnp.sum(ex * pg, axis=0, keepdims=True)
         for n, value in enumerate((top, total, weighted)):
-            stat_row[n, pl.ds(h, 1), :] = value
-
-    owner = lax.rem(iota((seq_count, STRIDE), 0), tiles) == iota((seq_count, STRIDE), 1) // TILE
-    code_row = lax.rem(iota((STRIDE, HEAD_DIM), 0), TILE)
-    code_row = lax.rem(code_row, 2) * HALF + code_row // 2
-    pick_lane = iota((STRIDE, HEAD_DIM), 1)
-    code_col = lax.rem(iota((HEAD_DIM, STRIDE), 1), TILE)
-    code_col = lax.rem(code_col, 2) * HALF + code_col // 2
-    pick_row = iota((HEAD_DIM, STRIDE), 0)
-
-    coded = jnp.zeros((seq_count, HEAD_DIM), F32)
-    for n in range(3):
-        values = jnp.broadcast_to(
-            stat_row[n][:, None, :], (heads, tiles, STRIDE)
-        ).reshape(seq_count, STRIDE)
-        select = (pick_lane == code_row + n * PAIRS).astype(F32)
-        coded = coded + dot_exact(jnp.where(owner, values, 0.0), select)
-    stat_snd[:, 0, :] = coded
-    stat_rcv[s] = stat_snd[s]
-
-    @pl.loop(1, seq_count)
-    def _(i):
-        send(stat_snd, stat_rcv, 2, i)
+            part_row[part, n, h : h + 1, :] = value
+
+    for h in range(heads):
+        band_part(h, kv_ref[h, 0], kv_ref[h, 1], row <= col, e_diag, pg_diag, 0)
+    for at in passed:
+        halo_pass(at)
 
     swap_row = iota((STRIDE, STRIDE), 0)
     swap_col = iota((STRIDE, STRIDE), 1)
@@ -340,6 +311,41 @@
         class_row[p : p + 1, :] = top
         class_row[PAIRS + p : PAIRS + p + 1, :] = jnp.sum(ec, axis=0, keepdims=True)
 
+    halo_all.wait_recv()
+    for h in range(heads):
+        band_part(h, halo[h, 0], halo[h, 1], (row > col) & (s > 0), e_prev, pg_prev, 1)
+    tops = [part_row[part, 0] for part in range(2)]
+    stat_row[0] = jnp.maximum(*tops)
+    stat_row[1] = jnp.zeros_like(tops[0])
+    stat_row[2] = jnp.zeros_like(tops[0])
+    for part in range(2):
+        level = jnp.exp(tops[part] - stat_row[0])
+        for n in range(1, 3):
+            stat_row[n] += part_row[part, n] * level
+        part_row[part, 0] = level
+
+    owner = lax.rem(iota((seq_count, STRIDE), 0), tiles) == iota((seq_count, STRIDE), 1) // TILE
+    code_row = lax.rem(iota((STRIDE, HEAD_DIM), 0), TILE)
+    code_row = lax.rem(code_row, 2) * HALF + code_row // 2
+    pick_lane = iota((STRIDE, HEAD_DIM), 1)
+    code_col = lax.rem(iota((HEAD_DIM, STRIDE), 1), TILE)
+    code_col = lax.rem(code_col, 2) * HALF + code_col // 2
+    pick_row = iota((HEAD_DIM, STRIDE), 0)
+
+    coded = jnp.zeros((seq_count, HEAD_DIM), F32)
+    for n in range(3):
+        values = jnp.broadcast_to(
+            stat_row[n][:, None, :], (heads, tiles, STRIDE)
+        ).reshape(seq_count, STRIDE)
+        select = (pick_lane == code_row + n * PAIRS).astype(F32)
+        coded = coded + dot_exact(jnp.where(owner, values, 0.0), select)
+    stat_snd[:, 0, :] = coded
+    stat_rcv[s] = stat_snd[s]
+
+    @pl.loop(1, seq_count, unroll=UNROLL)
+    def _(i):
+        send(stat_snd, stat_rcv, 2, i)
+
     whole(gsnd, grcv, 1).wait_recv()
     sort_classes([lambda these: grcv[these]], 3)
     for p in range(PAIRS):
@@ -355,7 +361,7 @@
     )
     cstat_rcv[s] = cstat_snd[s]
 
-    @pl.loop(1, seq_count)
+    @pl.loop(1, seq_count, unroll=UNROLL)
     def _(i):
         send(cstat_snd, cstat_rcv, 3, i)
 
@@ -391,7 +397,7 @@
             )
     grad_rcv[s] = grad_snd[s]
 
-    @pl.loop(1, EARLY)
+    @pl.loop(1, EARLY, unroll=UNROLL)
     def _(i):
         send(grad_snd, grad_rcv, 4, i)
 
@@ -410,7 +416,7 @@
         )
         stat_row[0, h : h + 1, :] = factor
         stat_row[1, h : h + 1, :] = delta
-        probs = e_prev[h] * factor
+        probs = e_prev[h] * (factor * part_row[1, 0, h : h + 1, :])
         sgrad = (probs * (pg_prev[h] - delta)).astype(BF16)
         back_snd[h, 0] = (dot_nn(sgrad, q_ref[h]) * SCALE).astype(BF16)
         back_snd[h, 1] = dot_nn(probs.astype(BF16), g_home[:, head_lanes(h)]).astype(BF16)
@@ -420,7 +426,7 @@
 
     def band_own(h):
         factor, delta = (stat_row[n, h : h + 1, :] for n in range(2))
-        probs = e_diag[h] * factor
+        probs = e_diag[h] * (factor * part_row[0, 0, h : h + 1, :])
         sgrad = (probs * (pg_diag[h] - delta)).astype(BF16)
         acc[0, h] = (acc[0, h] + dot_tn(sgrad, kv_ref[h, 0])) * SCALE
         acc[1, h] = dot_nn(sgrad, q_ref[h]) * SCALE
@@ -429,7 +435,7 @@
     for h in range(direct, heads):
         band_prev(h)
 
-    @pl.loop(EARLY, seq_count)
+    @pl.loop(EARLY, seq_count, unroll=UNROLL)
     def _(i):
         send(grad_snd, grad_rcv, 4, i)
 
@@ -441,15 +447,19 @@
             back_pass(at)
 
     whole(grad_snd, grad_rcv, 4).wait_recv()
-    back_all.wait_recv()
-    for h in range(heads):
-        for j, out in enumerate((dq_ref, dk_ref, dv_ref)):
+    for j in range(3):
+        for h in range(heads):
             value = acc[j, h] + grad_rcv[h * tiles : (h + 1) * tiles, j].reshape(
                 STRIDE, HEAD_DIM
             ).astype(F32)
-            if j > 0:
-                value = value + back_rcv[h, j - 1].astype(F32)
-            out[:, head_lanes(h)] = value.astype(BF16)
+            if j == 0:
+                out_ref[0, :, head_lanes(h)] = value.astype(BF16)
+            else:
+                acc[j, h] = value
+    back_all.wait_recv()
+    for h in range(heads):
+        for j in range(2):
+            out_ref[1 + j, :, head_lanes(h)] = (acc[1 + j, h] + back_rcv[h, j].astype(F32)).astype(BF16)
 
     for copy in g_copies:
         copy.wait_send()
@@ -484,9 +494,9 @@
     pair = 2 * seq_count
     grads = pl.pallas_call(
         functools.partial(kernel, seq_count, head_count),
-        out_shape=[pltpu.VMEM(queries.shape, BF16)] * 3,
+        out_shape=pltpu.VMEM((3,) + queries.shape, BF16),
         in_specs=[far] * 4,
-        out_specs=[vmem] * 3,
+        out_specs=vmem,
         scratch_shapes=[
             pltpu.VMEM((heads, length, HEAD_DIM), BF16),
             pltpu.VMEM((heads, 2, length, HEAD_DIM), BF16),
@@ -516,6 +526,7 @@
             pltpu.VMEM((heads, STRIDE, STRIDE), F32),
             pltpu.VMEM((heads, STRIDE, STRIDE), F32),
             pltpu.VMEM((heads, STRIDE, STRIDE), F32),
+            pltpu.VMEM((2, 3, heads, STRIDE), F32),
             pltpu.VMEM((3, heads, STRIDE), F32),
             pltpu.VMEM((3, heads, STRIDE), F32),
             pltpu.VMEM((3, heads, length, HEAD_DIM), F32),
@@ -536,7 +547,7 @@
             collective_id=0, has_side_effects=True, vmem_limit_bytes=62 * 2**20
         ),
     )(queries, keys, values, out_grad)
-    return grads
+    return grads[0], grads[1], grads[2]
 
 
 def solution(mesh):

time: 78.5 us -> 73.4 us (0.935)
  Pallas kernels: 75.6 us -> 71.7 us
  local copies, waits for them, and re-layouts: 2.11 us -> 0.89 us
    pallas_call x1, Pallas kernels: 75.6 us -> 71.7 us  [per_device(): pl.pallas_call(functools.partial(kernel, seq_count, head_count), out_shap...]
    unnamed x3 -> x0, local copies, waits for them, and re-layouts: 2.11 us -> none
    squeeze x0 -> x1, local copies, waits for them, and re-layouts: none -> 0.89 us  [per_device(): return (grads[0], grads[1], grads[2])]
where the time goes in v4:
time: 73.4 us; the launch traced here: 73.2 us
  Pallas kernels  71.7 us (98%)
  local copies, waits for them, and re-layouts  0.89 us (1%)
    pallas_call x1, Pallas kernels, per_device(): pl.pallas_call(functools.partial(kernel, seq_count, head_count), out_shap...  71.7 us

profile of v4, /device:TPU:24, one launch (start us, length us, event | category | flops | bytes accessed | tf_op | source)
XLA Modules:
  0.0 73.2 jit_solution(17397738831274626013)
XLA Ops:
  0.6 71.7 %shard_map.67 = bf16[3,256,512]{2,1,0:T(8,128)(2,1)S(1)} custom-call(bf16[256,512]{1,0:T(8,128)(2,1)} %q_hbm.1, bf16[256,512]{1,0:T(8,128)(2,1)} %k_hbm.1, bf16[256,512]{1,0:T(8,128)(2,1)} %v_hbm.1, bf16[64,2048]{1,0:T(8,128)(2,1)} %og_hbm.1), custom_call_target="tpu_custom_call" | custom-call | tf_op jit(solution)/shard_map/pallas_call | solution.py:495
  72.3 0.9 %slice_bitcast_fusion = (bf16[256,512]{1,0:T(8,128)(2,1)}, bf16[256,512]{1,0:T(8,128)(2,1)}, bf16[256,512]{1,0:T(8,128)(2,1)}) fusion(bf16[3,256,512]{2,1,0:T(8,128)(2,1)S(1)} %shard_map.67), kind=kLoop, calls=%fused_computation | loop fusion | bytes 1572864 | tf_op jit(solution)/shard_map/squeeze | solution.py:550

commit v5 on v4

--- a/solution.py
+++ b/solution.py
@@ -239,6 +239,9 @@
         def _(i):
             send(snd, rcv, 0, i)
 
+    for at in passed[:2]:
+        halo_pass(at)
+
     for copy in g_copies:
         copy.wait_recv()
     for h in range(heads):
@@ -268,7 +271,7 @@
 
     for h in range(heads):
         band_part(h, kv_ref[h, 0], kv_ref[h, 1], row <= col, e_diag, pg_diag, 0)
-    for at in passed:
+    for at in passed[2:]:
         halo_pass(at)
 
     swap_row = iota((STRIDE, STRIDE), 0)

time: 73.4 us -> 72.8 us (level)
  no operation moved by 1% of the time
where the time goes in v5:
time: 72.8 us; the launch traced here: 72.7 us
  Pallas kernels  71.2 us (98%)
  local copies, waits for them, and re-layouts  0.89 us (1%)
    pallas_call x1, Pallas kernels, per_device(): pl.pallas_call(functools.partial(kernel, seq_count, head_count), out_shap...  71.2 us

profile of v5, /device:TPU:24, one launch (start us, length us, event | category | flops | bytes accessed | tf_op | source)
XLA Modules:
  0.0 72.7 jit_solution(16521095435699139924)
XLA Ops:
  0.6 71.2 %shard_map.67 = bf16[3,256,512]{2,1,0:T(8,128)(2,1)S(1)} custom-call(bf16[256,512]{1,0:T(8,128)(2,1)} %q_hbm.1, bf16[256,512]{1,0:T(8,128)(2,1)} %k_hbm.1, bf16[256,512]{1,0:T(8,128)(2,1)} %v_hbm.1, bf16[64,2048]{1,0:T(8,128)(2,1)} %og_hbm.1), custom_call_target="tpu_custom_call" | custom-call | tf_op jit(solution)/shard_map/pallas_call | solution.py:498
  71.8 0.9 %slice_bitcast_fusion = (bf16[256,512]{1,0:T(8,128)(2,1)}, bf16[256,512]{1,0:T(8,128)(2,1)}, bf16[256,512]{1,0:T(8,128)(2,1)}) fusion(bf16[3,256,512]{2,1,0:T(8,128)(2,1)S(1)} %shard_map.67), kind=kLoop, calls=%fused_computation | loop fusion | bytes 1572864 | tf_op jit(solution)/shard_map/squeeze | solution.py:553

commit v6 on v5

--- a/solution.py
+++ b/solution.py
@@ -444,10 +444,10 @@
 
     for h in range(direct):
         band_prev(h)
+    for at in passed:
+        back_pass(at)
     for h in range(heads):
         band_own(h)
-        for at in passed[h * len(passed) // heads : (h + 1) * len(passed) // heads]:
-            back_pass(at)
 
     whole(grad_snd, grad_rcv, 4).wait_recv()
     for j in range(3):

time: 72.8 us -> 72.8 us (level)
  no operation moved by 1% of the time
where the time goes in v6:
time: 72.8 us; the launch traced here: 72.7 us
  Pallas kernels  71.2 us (98%)
  local copies, waits for them, and re-layouts  0.89 us (1%)
    pallas_call x1, Pallas kernels, per_device(): pl.pallas_call(functools.partial(kernel, seq_count, head_count), out_shap...  71.2 us

profile of v6, /device:TPU:24, one launch (start us, length us, event | category | flops | bytes accessed | tf_op | source)
XLA Modules:
  0.0 72.7 jit_solution(11817106845955638695)
XLA Ops:
  0.6 71.2 %shard_map.67 = bf16[3,256,512]{2,1,0:T(8,128)(2,1)S(1)} custom-call(bf16[256,512]{1,0:T(8,128)(2,1)} %q_hbm.1, bf16[256,512]{1,0:T(8,128)(2,1)} %k_hbm.1, bf16[256,512]{1,0:T(8,128)(2,1)} %v_hbm.1, bf16[64,2048]{1,0:T(8,128)(2,1)} %og_hbm.1), custom_call_target="tpu_custom_call" | custom-call | tf_op jit(solution)/shard_map/pallas_call | solution.py:498
  71.8 0.9 %slice_bitcast_fusion = (bf16[256,512]{1,0:T(8,128)(2,1)}, bf16[256,512]{1,0:T(8,128)(2,1)}, bf16[256,512]{1,0:T(8,128)(2,1)}) fusion(bf16[3,256,512]{2,1,0:T(8,128)(2,1)S(1)} %shard_map.67), kind=kLoop, calls=%fused_computation | loop fusion | bytes 1572864 | tf_op jit(solution)/shard_map/squeeze | solution.py:553

commit v7 on v6

--- a/solution.py
+++ b/solution.py
@@ -364,7 +364,7 @@
     )
     cstat_rcv[s] = cstat_snd[s]
 
-    @pl.loop(1, seq_count, unroll=UNROLL)
+    @pl.loop(1, seq_count, unroll=True)
     def _(i):
         send(cstat_snd, cstat_rcv, 3, i)
 

time: 72.8 us -> 72.8 us (level)
  no operation moved by 1% of the time
where the time goes in v7:
time: 72.8 us; the launch traced here: 72.7 us
  Pallas kernels  71.2 us (98%)
  local copies, waits for them, and re-layouts  0.89 us (1%)
    pallas_call x1, Pallas kernels, per_device(): pl.pallas_call(functools.partial(kernel, seq_count, head_count), out_shap...  71.2 us

profile of v7, /device:TPU:24, one launch (start us, length us, event | category | flops | bytes accessed | tf_op | source)
XLA Modules:
  0.0 72.7 jit_solution(6811048820151748688)
XLA Ops:
  0.6 71.2 %shard_map.67 = bf16[3,256,512]{2,1,0:T(8,128)(2,1)S(1)} custom-call(bf16[256,512]{1,0:T(8,128)(2,1)} %q_hbm.1, bf16[256,512]{1,0:T(8,128)(2,1)} %k_hbm.1, bf16[256,512]{1,0:T(8,128)(2,1)} %v_hbm.1, bf16[64,2048]{1,0:T(8,128)(2,1)} %og_hbm.1), custom_call_target="tpu_custom_call" | custom-call | tf_op jit(solution)/shard_map/pallas_call | solution.py:498
  71.8 0.9 %slice_bitcast_fusion = (bf16[256,512]{1,0:T(8,128)(2,1)}, bf16[256,512]{1,0:T(8,128)(2,1)}, bf16[256,512]{1,0:T(8,128)(2,1)}) fusion(bf16[3,256,512]{2,1,0:T(8,128)(2,1)S(1)} %shard_map.67), kind=kLoop, calls=%fused_computation | loop fusion | bytes 1572864 | tf_op jit(solution)/shard_map/squeeze | solution.py:553
